TPU v7x, 32 devices: a whole 2x2x4 slice. The times are simulated.
32 devices in a mesh: brow: 4 (over y, x), bcol: 8 (over z, core).
Axes of the slice: x: 2, y: 2, z: 4, core: 2. Of those that a mesh axis runs over, the one named last changes fastest.
Arguments:
- panel_points: bfloat16 [3, 6144], P(None, ('brow', 'bcol')), may hold values from 0 to 1
- panel_map: int32 [3, 6144], replicated, may hold values from 0 to 2047, as said below
- element_nodes: int32 [125, 1024], P(None, ('brow', 'bcol')), may hold values from 0 to 2047
- element_coef: float32 [1024], P(('brow', 'bcol')), may hold values from 0.1 to 1
- element_matrix: float32 [125, 125], replicated, as said below
- node_mass: float32 [65536], P(('brow', 'bcol')), may hold values from 2 to 4
- forcing: float32 [64, 65536], P(None, ('brow', 'bcol')), may hold values from -6 to 6
- field_start: float32 [64, 65536], P(None, ('brow', 'bcol')), may hold values from -6 to 6
- potential_start: float32 [64, 6144], P(None, ('brow', 'bcol')), may hold values from -6 to 6
Outputs:
- fem_field: float32 [64, 65536], P(None, ('brow', 'bcol'))
- potential: float32 [64, 6144], P(None, ('brow', 'bcol'))
Inputs may be any that keep to these rules, and one draw needn't show every extreme that they name: `panel_map`: row 0 is an index over brow+bcol (brow slowest), row 2 a local node below 2048. In each aligned block of 192 panels every group owns either no panel or exactly 12 of them, whose row 1 values are 0 to 11, each once. `element_nodes`: local node numbers within the element's own group. `element_matrix`: Symmetric.
All inputs are finite; a program needn't handle non-finite values.
Results may differ from a plain program's by a relative error of at most 0.0015.
The roundings to bfloat16 on the way count: a program that leaves them out, or rounds other values in their place, can miss the bound.
Values may be sent and summed in bfloat16 or wider, within the bound.
No kernel may reach another device: no remote copies, remote signals or barrier semaphores. Data moves between devices by JAX's collectives and lax.ppermute only.
A program may use at most 128 MiB of HBM per device.

v0:
```python
import functools
import math

import jax
import jax.numpy as jnp
from jax import lax
from jax.experimental import pallas as pl
from jax.experimental.pallas import tpu as pltpu
from jax.sharding import PartitionSpec as P

RIM = 128
SWEEPS = 3
LANES = 128
LOAD_ROWS = 8
POINT_ROWS = 8
HALVES = 2
GROUP = 4
BLOCKS = 4

wave_number = 20.0
penalty = 0.5

AXES = ("brow", "bcol")
F32 = jnp.float32
BF16 = jnp.bfloat16

SIN_POLY = (3.14159264, -5.16771008, 2.55007752, -0.59829129, 0.07765766)

ROUNDER = 1.5 * 2.0**23
MIB = 1024 * 1024


def weight_of(sweep):
    return 1.0 / (1.25 + 0.75 * math.cos(math.pi * (2 * sweep + 1) / (2.0 * SWEEPS)))


def call(kernel, out_shape, cost, limit=28, **more):
    return pl.pallas_call(
        kernel,
        out_shape=out_shape,
        compiler_params=pltpu.CompilerParams(vmem_limit_bytes=limit * MIB),
        cost_estimate=pl.CostEstimate(flops=cost, bytes_accessed=1 << 20, transcendentals=0),
        **more,
    )


def shape_of(shape, dtype):
    return jax.ShapeDtypeStruct(shape, dtype)


def kept(shape, dtype):
    return pltpu.VMEM(shape, dtype)


def in_hbm(*arrays):
    return tuple(pltpu.with_memory_space_constraint(array, pltpu.HBM) for array in arrays)


def in_vmem(*arrays):
    return tuple(pltpu.with_memory_space_constraint(array, pltpu.VMEM) for array in arrays)


def dot(a, b):
    return jnp.dot(a, b, preferred_element_type=F32)


def dot_nt(a, b):
    return lax.dot_general(a, b, (((1,), (1,)), ((), ())), preferred_element_type=F32)


def split_two(value):
    high = value.astype(BF16)
    return high, (value - high.astype(F32)).astype(BF16)


def low_part(value, size):
    return value & (size - 1) if size & (size - 1) == 0 else value % size


def high_part(value, size):
    return value >> (size.bit_length() - 1) if size & (size - 1) == 0 else value // size


def stack_parts(value, parts):
    width = value.shape[1] // parts
    return jnp.concatenate([value[:, i * width : (i + 1) * width] for i in range(parts)], axis=0)


def one_hot_rows(key, rows):
    seen = lax.broadcasted_iota(jnp.int16, (rows, key.shape[1]), 0)
    return jnp.where(seen == key.astype(jnp.int16), BF16(1), BF16(0))


def pick_part(stacked, part, parts):
    rows = stacked.shape[0] // parts
    picked = stacked[(parts - 1) * rows :]
    for i in reversed(range(parts - 1)):
        picked = jnp.where(part == i, stacked[i * rows : (i + 1) * rows], picked)
    return picked


def gather_nodes(field, nodes, parts):
    width = field.shape[1] // parts
    hot = one_hot_rows(jnp.where(nodes < 0, -1, low_part(nodes, width)), width)
    found = dot(stack_parts(field.astype(BF16), parts), hot)
    return pick_part(found, high_part(nodes, width), parts)


def scatter_nodes(values, nodes, parts, count):
    width = count // parts
    hot = one_hot_rows(jnp.where(nodes < 0, -1, low_part(nodes, width)), width)
    masked = jnp.concatenate(
        [jnp.where(high_part(nodes, width) == i, values, 0.0) for i in range(parts)], axis=0
    ).astype(BF16)
    added = dot_nt(masked, hot)
    rows = values.shape[0]
    return jnp.concatenate([added[i * rows : (i + 1) * rows] for i in range(parts)], axis=1)


def halves_of(slot, rows):
    half = jnp.where(slot >= rows, 1, 0)
    return half, slot - half * rows


def trace_rows(field, nodes, parts, groups, used):
    turned = jnp.transpose(gather_nodes(field, nodes, parts))
    pieces = []
    for group in range(groups):
        base = group * HALVES * used
        pieces.append(
            jnp.concatenate([turned[base : base + used], turned[base + used : base + 2 * used]], axis=1)
        )
    return pieces


def own_panels(map_ref, rank, panel_dev):
    first = rank * panel_dev
    base = (first >> 7) << 7
    window = -(-panel_dev // LANES) * LANES
    near = map_ref[:, pl.ds(pl.multiple_of(base, LANES), window)]
    return jnp.where(first == base, near[:, :panel_dev], near[:, window - panel_dev :])


def load_rows(potential, own_map, devices, slot_rows):
    owner, slot = own_map[0:1], own_map[1:2]
    half, low = halves_of(slot, slot_rows)
    rows = devices * LOAD_ROWS
    key = half * rows + owner * LOAD_ROWS + low
    found = dot_nt(one_hot_rows(key, HALVES * rows), potential.astype(BF16))
    return jnp.concatenate([found[:rows], found[rows:]], axis=1).reshape(devices, LOAD_ROWS, LANES)


def node_tables(map_ref, rank, brow, bcol, panel_dev, slot_rows):
    row_panels = bcol * panel_dev
    trace_slots, load_slots = table_lanes(brow, bcol, slot_rows)
    lane = lax.broadcasted_iota(jnp.int32, (1, row_panels), 1).astype(F32)
    block = jnp.floor((lane + 0.5) * (1.0 / panel_dev)).astype(jnp.int32)
    row_id = lax.broadcasted_iota(jnp.int32, (8, row_panels), 0)
    loads = []
    for r in range(brow):
        span = slice(r * row_panels, (r + 1) * row_panels)
        owner, slot, node = map_ref[0:1, span], map_ref[1:2, span], map_ref[2:3, span]
        half, low = halves_of(slot, slot_rows)
        values = jnp.where(
            row_id == 0, high_part(node, 256), jnp.where(row_id == 1, low_part(node, 256), 1)
        ).astype(F32).astype(BF16)
        key = jnp.where(owner == rank, (half * bcol + block) * LOAD_ROWS + low, -1)
        loads.append(dot_nt(values, one_hot_rows(key, load_slots // brow)))
    loads = jnp.concatenate(loads, axis=1)
    place = lax.broadcasted_iota(jnp.int32, (1, load_slots), 1)
    row, inside = place // (load_slots // brow), place % (load_slots // brow)
    half, inside = inside // (bcol * LOAD_ROWS), inside % (bcol * LOAD_ROWS)
    column, low = inside // LOAD_ROWS, inside % LOAD_ROWS
    key = ((column * HALVES + half) * brow + row) * slot_rows + low
    key = jnp.where((low < slot_rows) & (half < HALVES), key, -1)
    traces = dot_nt(loads.astype(BF16), one_hot_rows(key, trace_slots))
    tables = []
    for found in (traces, loads):
        table = jnp.where(found[2:3] > 0.5, found[0:1] * 256.0 + found[1:2], -1.0)
        tables.append(table.astype(jnp.int32))
    return tables


def table_lanes(brow, bcol, slot_rows):
    trace_slots = -(-HALVES * brow * bcol * slot_rows // LANES) * LANES
    return trace_slots, brow * (-(-HALVES * bcol * LOAD_ROWS // LANES) * LANES)


def point_rows(points):
    row_id = lax.broadcasted_iota(jnp.int32, (POINT_ROWS, LANES), 0)
    each = POINT_ROWS // 3
    width = points.shape[1]
    value = jnp.zeros((POINT_ROWS, LANES), F32)
    for axis in range(3):
        for part in range(-(-width // LANES)):
            piece = points[axis : axis + 1, part * LANES : (part + 1) * LANES]
            short = LANES - piece.shape[1]
            if short:
                piece = jnp.concatenate([piece, jnp.zeros((1, short), F32)], axis=1)
            value = jnp.where(row_id == axis * each + part, piece, value)
    return value


def write_chunks(chunk_ref, pieces, loads, points=None):
    used = pieces[0].shape[0]
    for device in range(chunk_ref.shape[0]):
        rows = [pieces[device % len(pieces)], loads[device]] + ([] if points is None else [points])
        left = chunk_ref.shape[1] - sum(piece.shape[0] for piece in rows)
        if left:
            rows.append(jnp.zeros((left, LANES), F32))
        chunk_ref[device] = jnp.concatenate(rows, axis=0).astype(BF16)


def write_rims(field, even, first_ref, second_ref):
    low = field[:, :RIM]
    high = field[:, field.shape[1] - RIM :]
    first_ref[...] = jnp.where(even, high, low).astype(BF16)
    second_ref[...] = jnp.where(even, low, high).astype(BF16)


def setup_kernel(
    parts, brow, bcol, panel_dev, slot_rows, rank_ref, map_ref, field_ref, potential_ref, points_ref,
    element_nodes_ref, element_matrix_ref, node_mass_ref,
    nodes_ref, load_nodes_ref, source_map_ref, own_map_ref, keys_ref, matrix_ref, mass_ref,
    chunk_ref, rim_first_ref, rim_second_ref,
):
    rank = rank_ref[0]
    source_map_ref[...] = jnp.concatenate(
        [
            own_panels(map_ref, r * bcol + low_part(rank, bcol), panel_dev)
            for r in range(brow)
        ],
        axis=1,
    )
    own_map = own_panels(map_ref, rank, panel_dev)
    own_map_ref[...] = own_map
    keys_ref[...] = jnp.zeros_like(keys_ref)
    keys_ref[:, : element_nodes_ref.shape[1]] = element_nodes_ref[...]
    matrix_ref[...] = jnp.zeros_like(matrix_ref)
    matrix_ref[: element_matrix_ref.shape[0], : element_matrix_ref.shape[1]] = element_matrix_ref[...]
    mass_ref[...] = node_mass_ref[...]
    nodes, load_nodes = node_tables(map_ref, rank, brow, bcol, panel_dev, slot_rows)
    nodes_ref[...] = jnp.broadcast_to(nodes, nodes_ref.shape)
    load_nodes_ref[...] = jnp.broadcast_to(load_nodes, load_nodes_ref.shape)
    field = field_ref[...]
    write_rims(field, low_part(rank, 2) == 0, rim_first_ref, rim_second_ref)
    loads = load_rows(potential_ref[...], own_map, brow * bcol, slot_rows)
    pieces = trace_rows(field, nodes, parts, bcol, brow * slot_rows)
    write_chunks(chunk_ref, pieces, loads, point_rows(points_ref[...].astype(F32)))


def rim_correction(value, even, first_ref, second_ref, mass, weight):
    step = weight * penalty
    first, second = first_ref[...].astype(F32), second_ref[...].astype(F32)
    left, right = jnp.where(even, second, first), jnp.where(even, first, second)
    last = value.shape[1] - RIM
    low = value[:, :RIM] + left * (step / mass[:, :RIM])
    high = value[:, last:] + right * (step / mass[:, last:])
    return jnp.concatenate([low, value[:, RIM:last], high], axis=1)


def received_loads(chunk_ref, used, brow, columns):
    received = chunk_ref[...].astype(F32)[:, used : used + LOAD_ROWS]
    received = received.reshape(received.shape[0] * LOAD_ROWS, LANES)
    span = received.shape[0] // brow
    rows = []
    for r in range(brow):
        piece = received[r * span : (r + 1) * span]
        rows += [piece[:, :columns], piece[:, columns : HALVES * columns]]
    return jnp.transpose(jnp.concatenate(rows, axis=0))


def sweep_kernel(
    parts, weight, weight_before, keep, rank_ref, coef_ref, field_ref, rhs_ref, mass_ref, keys_ref,
    matrix_ref, *more_refs,
):
    if keep:
        out_ref, kept_ref, sem, *scratch = more_refs
        copy = pltpu.make_async_copy(rhs_ref, kept_ref, sem)
        copy.start()
        rhs_ref = kept_ref
    elif weight_before is None:
        out_ref, *scratch = more_refs
    else:
        first_ref, second_ref, out_ref, field_scr, *scratch = more_refs
    hot_ref, high_ref, low_ref, found_ref, local_ref, product_ref, yhigh_ref, ylow_ref, sum_ref = scratch
    groups = hot_ref.shape[0]
    columns, count = field_ref.shape
    width = count // parts
    mass = mass_ref[...]
    if weight_before is None:
        field = field_ref[...]
        field_now = field_ref
    else:
        even = low_part(rank_ref[0], 2) == 0
        field = rim_correction(field_ref[...], even, first_ref, second_ref, mass, weight_before)
        field_scr[...] = field
        field_now = field_scr
    high, low = split_two(field)
    for h in range(parts):
        high_ref[h * columns : (h + 1) * columns] = high[:, h * width : (h + 1) * width]
        low_ref[h * columns : (h + 1) * columns] = low[:, h * width : (h + 1) * width]
    mat_high, mat_low = split_two(matrix_ref[...])
    matrix = jnp.concatenate(
        [
            jnp.concatenate([mat_high, mat_low], axis=1),
            jnp.concatenate([mat_high, jnp.zeros_like(mat_low)], axis=1),
        ],
        axis=0,
    )

    def build(group):
        for e in range(GROUP):
            key = keys_ref[group * GROUP + e : group * GROUP + e + 1, :]
            hot_ref[group, :, e * LANES : (e + 1) * LANES] = one_hot_rows(low_part(key, width), width)

    def gather(group):
        hot = hot_ref[group]
        found_ref[group % 2] = dot(high_ref[...], hot) + dot(low_ref[...], hot)

    def pick(group):
        slot = group % 2
        for e in range(GROUP):
            element = group * GROUP + e
            key = keys_ref[element : element + 1, :]
            got = pick_part(found_ref[slot, :, e * LANES : (e + 1) * LANES], high_part(key, width), parts)
            got_high, got_low = split_two(got)
            local_ref[slot, e * columns : (e + 1) * columns, :LANES] = got_high
            local_ref[slot, e * columns : (e + 1) * columns, LANES:] = got_low


    def multiply(group):
        product_ref[group % 2] = dot(local_ref[group % 2], matrix)

    def scale(group):
        slot = group % 2
        for e in range(GROUP):
            element = group * GROUP + e
            part = high_part(keys_ref[element : element + 1, :], width)
            rows = product_ref[slot, e * columns : (e + 1) * columns]
            value = (rows[:, :LANES] + rows[:, LANES:]) * coef_ref[element]
            value_high, value_low = split_two(value)
            span = slice(e * LANES, (e + 1) * LANES)
            for h in range(parts):
                mask = jnp.where(part == h, 1.0, 0.0).astype(BF16)
                yhigh_ref[slot, h * columns : (h + 1) * columns, span] = value_high * mask
                ylow_ref[slot, h * columns : (h + 1) * columns, span] = value_low * mask

    def scatter(group):
        hot = hot_ref[group]
        added = dot_nt(yhigh_ref[group % 2], hot) + dot_nt(ylow_ref[group % 2], hot)
        sum_ref[...] = added if group == 0 else sum_ref[...] + added

    build(0)
    gather(0)
    build(1)
    for group in range(groups):
        pick(group)
        if group + 1 < groups:
            gather(group + 1)
        if group + 2 < groups:
            build(group + 2)
        multiply(group)
        if group:
            scatter(group - 1)
        scale(group)
    scatter(groups - 1)
    if keep:
        copy.wait()
    for h in range(parts):
        span = slice(h * width, (h + 1) * width)
        stiff = sum_ref[h * columns : (h + 1) * columns]
        out_ref[:, span] = (1.0 - weight) * field_now[:, span] + (rhs_ref[:, span] - stiff) * (
            weight / mass[:, span]
        )


def loads_kernel(
    parts, brow, weight, used, rank_ref, nodes_ref, chunk_ref, forcing_ref, field_ref, first_ref,
    second_ref, mass_ref, rhs_ref, out_ref, rim_first_ref, rim_second_ref,
):
    columns, count = field_ref.shape
    loads = received_loads(chunk_ref, used, brow, columns)
    added = scatter_nodes(loads, nodes_ref[0:1, :], parts, count)
    rhs_ref[...] = forcing_ref[...] + added
    mass = mass_ref[...]
    even = low_part(rank_ref[0], 2) == 0
    field = field_ref[...] + added * (weight / mass)
    field = rim_correction(field, even, first_ref, second_ref, mass, weight)
    out_ref[...] = field
    write_rims(field, even, rim_first_ref, rim_second_ref)


def total(parts_ref):
    value = parts_ref[0]
    for r in range(1, parts_ref.shape[0]):
        value = value + parts_ref[r]
    return value


def finish_kernel(
    parts, brow, bcol, panel_dev, slot_rows, weight, rank_ref, own_map_ref, nodes_ref, field_ref,
    first_ref, second_ref, mass_ref, parts_ref, out_ref, chunk_ref, rim_first_ref, rim_second_ref,
):
    rank = rank_ref[0]
    even = low_part(rank, 2) == 0
    field = rim_correction(field_ref[...], even, first_ref, second_ref, mass_ref[...], weight)
    out_ref[...] = field
    write_rims(field, even, rim_first_ref, rim_second_ref)
    loads = load_rows(total(parts_ref), own_map_ref[...], brow * bcol, slot_rows)
    pieces = trace_rows(field, nodes_ref[0:1, :], parts, bcol, brow * slot_rows)
    write_chunks(chunk_ref, pieces, loads)


def last_kernel(
    weight, rank_ref, field_ref, first_ref, second_ref, mass_ref, parts_ref, out_ref, potential_ref
):
    even = low_part(rank_ref[0], 2) == 0
    out_ref[...] = rim_correction(field_ref[...], even, first_ref, second_ref, mass_ref[...], weight)
    potential_ref[...] = total(parts_ref)


def density_groups(map_ref, chunk_ref, brow, bcol, panel_dev, slot_rows):
    devices = brow * bcol
    columns = LANES // HALVES
    rows = BLOCKS * slot_rows
    panels = BLOCKS * panel_dev
    lane = lax.broadcasted_iota(jnp.int32, (1, panels), 1).astype(F32)
    block = jnp.floor((lane + 0.5) * (1.0 / panel_dev)).astype(jnp.int32)
    traces = chunk_ref[...].astype(F32)
    for group in range(brow // BLOCKS):
        span = slice(group * panels, (group + 1) * panels)
        owner, slot = map_ref[0:1, span], map_ref[1:2, span]
        half, low = halves_of(slot, slot_rows)
        key = owner * rows + block * slot_rows + low
        near = traces[:, group * rows : (group + 1) * rows].reshape(devices * rows, LANES)
        found = dot(jnp.transpose(near).astype(BF16), one_hot_rows(key, devices * rows))
        density = jnp.where(half == 0, found[:columns], found[columns:])
        turned = jnp.concatenate([-density[columns // 2 :], density[: columns // 2]], axis=0)
        yield density.astype(BF16), turned.astype(BF16)


def write_parts(out_ref, total, panel_dev):
    for r in range(out_ref.shape[0]):
        out_ref[r] = total[:, r * panel_dev : (r + 1) * panel_dev]


def split_three(value):
    high = value.astype(BF16).astype(F32)
    middle = (value - high).astype(BF16).astype(F32)
    return [high, middle, value - high - middle]


def squares(axes):
    return sum(row * row for row in axes[1:]) + axes[0] * axes[0]


def rows_of(rows, dtype=BF16):
    row_id = lax.broadcasted_iota(jnp.int32, (16, rows[0].shape[1]), 0)
    value = jnp.zeros(row_id.shape, F32)
    for index, row in enumerate(rows):
        value = jnp.where(row_id == index, row, value)
    return value.astype(dtype)


def tile_kernel(
    brow, bcol, panel_dev, slot_rows, rank_ref, map_ref, chunk_ref, out_ref, tile_ref,
    target_ref, density_ref, turned_ref, distance_ref, built_ref, sum_ref, sems,
):
    count_all = brow * bcol * panel_dev
    soften = 0.5 * float(count_all) ** (-1.0 / 3.0)
    each = POINT_ROWS // 3
    row_index, col_index = high_part(rank_ref[0], bcol), low_part(rank_ref[0], bcol)
    start = brow * slot_rows + LOAD_ROWS
    block = pl.program_id(0)

    def points_of(device):
        return chunk_ref[device].astype(F32)[start : start + POINT_ROWS]

    def copy_of(index):
        return pltpu.make_async_copy(built_ref.at[index], tile_ref.at[index], sems.at[index])

    @pl.when(block == 0)
    def prepare():
        near = [points_of(row_index * bcol + c) for c in range(bcol)]
        axes = []
        for axis in range(3):
            rows = []
            for piece in near:
                for part in range(each):
                    wide = min(LANES, panel_dev - part * LANES)
                    rows.append(piece[axis * each + part : axis * each + part + 1, :wide])
            axes.append(jnp.concatenate(rows, axis=1))
        norms = split_three(squares(axes) + soften * soften)
        target_ref[...] = rows_of([-2.0 * row for row in axes] + [jnp.ones_like(axes[0])] * 3 + norms)
        sum_ref[...] = jnp.zeros_like(sum_ref)
        groups = density_groups(map_ref, chunk_ref, brow, bcol, panel_dev, slot_rows)
        for group, (density, turned) in enumerate(groups):
            for k in range(BLOCKS):
                span = slice(k * panel_dev, (k + 1) * panel_dev)
                density_ref[group * BLOCKS + k] = density[:, span]
                turned_ref[group * BLOCKS + k] = turned[:, span]

    piece = points_of(block * bcol + col_index)
    axes = [
        jnp.concatenate([piece[axis * each + part : axis * each + part + 1] for part in range(each)], axis=1)
        for axis in range(3)
    ]
    norms = split_three(squares(axes))
    source = jnp.transpose(rows_of(axes + norms + [jnp.ones_like(axes[0])] * 3, F32)).astype(BF16)
    distance_ref[...] = dot(source[:panel_dev], target_ref[...])
    step, lanes = 16, 4 * LANES
    wide = distance_ref.shape[1]
    places = [
        (slice(top, top + step), slice(left, min(left + lanes, wide)))
        for top in range(0, panel_dev, step)
        for left in range(0, wide, lanes)
    ]
    for rows, span in places:
        squared = distance_ref[rows, span]
        inverse = lax.rsqrt(squared)
        turns = (squared * inverse) * (wave_number / (2.0 * math.pi))
        turns = turns - ((turns + ROUNDER) - ROUNDER)
        z = turns * turns
        sine = jnp.full_like(z, SIN_POLY[-1])
        for factor in SIN_POLY[-2::-1]:
            sine = sine * z + factor
        sine = sine * turns
        rest = 1.0 - sine * sine
        safe = jnp.maximum(rest, 1e-12)
        cosine = safe * lax.rsqrt(safe)
        double = inverse * (2.0 / math.sqrt(float(count_all)))
        built_ref[block, 0, rows, span] = ((rest - 0.5) * double).astype(BF16)
        built_ref[block, 1, rows, span] = (sine * cosine * double).astype(BF16)
    copy_of(block).start()
    sum_ref[...] += dot(density_ref[block], built_ref[block, 0]) + dot(
        turned_ref[block], built_ref[block, 1]
    )

    @pl.when(block == brow - 1)
    def end():
        write_parts(out_ref, sum_ref[...], panel_dev)
        for index in range(brow):
            copy_of(index).wait()


def potential_kernel(
    brow, bcol, panel_dev, slot_rows, map_ref, chunk_ref, tile_ref, out_ref, held_ref, sems,
):
    copies = [
        pltpu.make_async_copy(tile_ref.at[block], held_ref.at[block], sems.at[block])
        for block in range(brow)
    ]
    for copy in copies:
        copy.start()
    whole = None
    groups = density_groups(map_ref, chunk_ref, brow, bcol, panel_dev, slot_rows)
    for group, (density, turned) in enumerate(groups):
        for k in range(BLOCKS):
            block = group * BLOCKS + k
            copies[block].wait()
            span = slice(k * panel_dev, (k + 1) * panel_dev)
            part = dot(density[:, span], held_ref[block, 0]) + dot(turned[:, span], held_ref[block, 1])
            whole = part if whole is None else whole + part
    write_parts(out_ref, whole, panel_dev)


def per_device(
    panel_points,
    panel_map,
    element_nodes,
    element_coef,
    element_matrix,
    node_mass,
    forcing,
    field_start,
    potential_start,
):
    columns, panel_dev = potential_start.shape
    count = field_start.shape[1]
    brow, bcol = lax.axis_size("brow"), lax.axis_size("bcol")
    devices = brow * bcol
    capacity = max(2, 2 * panel_dev // devices)
    slot_rows = -(-capacity // HALVES)
    used = brow * slot_rows
    assert slot_rows <= LOAD_ROWS and columns * HALVES == LANES and brow % BLOCKS == 0
    parts = 256 // columns
    width = count // parts
    row_panels = bcol * panel_dev
    row_index, col_index = lax.axis_index("brow"), lax.axis_index("bcol")
    rank = (row_index * bcol + col_index).reshape(1)
    nodes_each, elements = element_nodes.shape
    assert elements % GROUP == 0
    smem = pl.BlockSpec(memory_space=pltpu.SMEM)
    vmem = pl.BlockSpec(memory_space=pltpu.VMEM)
    rim_shape = shape_of((columns, RIM), BF16)
    field_shape = shape_of((columns, count), F32)
    weights = [weight_of(sweep_index) for sweep_index in range(SWEEPS)]
    even_pairs = [(i, i ^ 1) for i in range(devices)]
    odd_pairs = [pair for i in range(1, devices - 1, 2) for pair in ((i, i + 1), (i + 1, i))]
    even = (rank[0] & 1) == 0

    def chunk_shape(rows, unit):
        return shape_of((devices, -(-rows // unit) * unit, LANES), BF16)

    def exchange(first, second):
        return lax.ppermute(first, AXES, even_pairs), lax.ppermute(second, AXES, odd_pairs)

    def rims(field, halo, weight):
        first, second = (piece.astype(F32) for piece in halo)
        left, right = jnp.where(even, second, first), jnp.where(even, first, second)
        last = count - RIM
        low = field[:, :RIM] + (weight * penalty) * left / mass[:, :RIM]
        high = field[:, last:] + (weight * penalty) * right / mass[:, last:]
        return jnp.where(even, high, low).astype(BF16), jnp.where(even, low, high).astype(BF16)

    def swap_all(chunks):
        return lax.all_to_all(chunks, AXES, split_axis=0, concat_axis=0, tiled=True)

    hbm = pl.BlockSpec(memory_space=pltpu.HBM)
    hot_shape = (elements // GROUP, width, GROUP * LANES)
    tile_shape = (brow, HALVES, panel_dev, bcol * panel_dev)

    def sweep(field, rhs, weight, halo=(), weight_before=None, keep=False):
        rows = parts * columns
        lanes = GROUP * LANES
        large = in_hbm(field, rhs) if keep else (field, rhs)
        given = (rank, *in_hbm(element_coef), *large, *in_vmem(mass, keys, matrix), *halo)
        return call(
            functools.partial(sweep_kernel, parts, weight, weight_before, keep),
            (field_shape, kept((columns, count), F32)) if keep else field_shape,
            5_000_000_000,
            in_specs=[smem, smem, vmem, hbm if keep else vmem] + [vmem] * (len(given) - 4),
            out_specs=(vmem, vmem) if keep else vmem,
            scratch_shapes=[pltpu.SemaphoreType.DMA] * keep
            + [pltpu.VMEM((columns, count), F32)] * bool(halo)
            + [
                pltpu.VMEM(hot_shape, BF16),
                pltpu.VMEM((rows, width), BF16),
                pltpu.VMEM((rows, width), BF16),
                pltpu.VMEM((2, rows, lanes), F32),
                pltpu.VMEM((2, GROUP * columns, 2 * LANES), BF16),
                pltpu.VMEM((2, GROUP * columns, 2 * LANES), F32),
                pltpu.VMEM((2, rows, lanes), BF16),
                pltpu.VMEM((2, rows, lanes), BF16),
                pltpu.VMEM((rows, width), F32),
            ],
        )(*given)

    def add_loads(chunks, field, halo, weight):
        return call(
            functools.partial(loads_kernel, parts, brow, weight, used),
            (field_shape, field_shape, rim_shape, rim_shape),
            500_000_000,
            in_specs=[smem] + [vmem] * 7,
            out_specs=(vmem,) * 4,
        )(rank, *in_vmem(load_nodes), chunks, *in_vmem(forcing_kept), field, *halo, *in_vmem(mass))

    parts_shape = shape_of((bcol, columns, panel_dev), F32)
    sizes = (brow, bcol, panel_dev, slot_rows)
    tile_mib = -(-(2 * math.prod(tile_shape)) // MIB)

    def swap_parts(parts_out):
        return lax.all_to_all(parts_out, "bcol", split_axis=0, concat_axis=0, tiled=True)

    trace_slots, load_slots = table_lanes(brow, bcol, slot_rows)
    (nodes, load_nodes, source_map, own_map, keys, matrix, mass, chunks, *rim) = call(
        functools.partial(setup_kernel, parts, brow, bcol, panel_dev, slot_rows),
        (
            kept((8, trace_slots), jnp.int32),
            kept((8, load_slots), jnp.int32),
            kept((3, brow * panel_dev), jnp.int32),
            kept((3, panel_dev), jnp.int32),
            kept((elements, LANES), jnp.int32),
            kept((LANES, LANES), F32),
            kept((1, count), F32),
            chunk_shape(used + LOAD_ROWS + POINT_ROWS, 8),
            kept(rim_shape.shape, BF16),
            kept(rim_shape.shape, BF16),
        ),
        2_000_000_000,
        in_specs=[smem] + [vmem] * 7,
        out_specs=(vmem,) * 10,
    )(
        rank,
        *in_hbm(
            panel_map, field_start, potential_start, panel_points, element_nodes.T, element_matrix,
            node_mass.reshape(1, count),
        ),
    )
    halo = exchange(*rim)
    chunks = swap_all(chunks)
    field, forcing_kept = sweep(field_start, forcing, weights[0], keep=True)
    parts_out, tiles = call(
        functools.partial(tile_kernel, *sizes),
        (parts_shape, pltpu.HBM(tile_shape, BF16)),
        8_000_000_000,
        grid=(brow,),
        limit=16 + tile_mib,
        in_specs=[smem, vmem, vmem],
        out_specs=(vmem, hbm),
        scratch_shapes=[
            pltpu.VMEM((16, bcol * panel_dev), BF16),
            pltpu.VMEM((brow, columns, panel_dev), BF16),
            pltpu.VMEM((brow, columns, panel_dev), BF16),
            pltpu.VMEM((panel_dev, bcol * panel_dev), F32),
            pltpu.VMEM(tile_shape, BF16),
            pltpu.VMEM((columns, bcol * panel_dev), F32),
            pltpu.SemaphoreType.DMA((brow,)),
        ],
    )(rank, *in_vmem(source_map), chunks)
    parts_in = swap_parts(parts_out)
    rhs, field, *rim = add_loads(chunks, field, halo, weights[0])
    halo = exchange(*rim)
    field = sweep(field, rhs, weights[1])
    halo_next = exchange(*rims(field, halo, weights[1]))
    field = sweep(field, rhs, weights[2], halo, weights[1])
    field, chunks, *rim = call(
        functools.partial(finish_kernel, parts, brow, bcol, panel_dev, slot_rows, weights[2]),
        (field_shape, chunk_shape(used + LOAD_ROWS, 8), rim_shape, rim_shape),
        1_000_000_000,
        in_specs=[smem] + [vmem] * 7,
        out_specs=(vmem,) * 4,
    )(rank, *in_vmem(own_map, nodes), field, *halo_next, *in_vmem(mass), parts_in)

    halo = exchange(*rim)
    chunks = swap_all(chunks)
    field = sweep(field, *in_vmem(forcing_kept), weights[0])
    parts_out = call(
        functools.partial(potential_kernel, *sizes),
        parts_shape,
        2_000_000_000,
        limit=16 + tile_mib,
        in_specs=[vmem, vmem, hbm],
        out_specs=vmem,
        scratch_shapes=[pltpu.VMEM(tile_shape, BF16), pltpu.SemaphoreType.DMA((brow,))],
    )(*in_vmem(source_map), chunks, *in_hbm(tiles))
    parts_in = swap_parts(parts_out)
    rhs, field, *rim = add_loads(chunks, field, halo, weights[0])
    halo = exchange(*rim)
    field = sweep(field, rhs, weights[1])
    halo_next = exchange(*rims(field, halo, weights[1]))
    field = sweep(field, rhs, weights[2], halo, weights[1])
    return call(
        functools.partial(last_kernel, weights[2]),
        (field_shape, shape_of((columns, panel_dev), F32)),
        100_000_000,
        in_specs=[smem] + [vmem] * 5,
        out_specs=(vmem, vmem),
    )(rank, field, *halo_next, *in_vmem(mass), parts_in)


def solution(mesh):
    placed = (
        P(None, AXES),
        P(),
        P(None, AXES),
        P(AXES),
        P(),
        P(AXES),
        P(None, AXES),
        P(None, AXES),
        P(None, AXES),
    )
    return jax.shard_map(
        per_device,
        mesh=mesh,
        in_specs=placed,
        out_specs=(P(None, AXES), P(None, AXES)),
        check_vma=False,
    )
```

profile of v0, /device:TPU:4, one launch (start us, length us, event | category | flops | bytes accessed | tf_op | source)
XLA Modules:
  0.0 104.0 jit_solution(9390346116343987613)
XLA Ops:
  0.6 3.0 %shard_map.104 = (s32[8,384]{1,0:T(8,128)S(1)}, s32[8,512]{1,0:T(8,128)S(1)}, s32[3,768]{1,0:T(4,128)S(1)}, s32[3,192]{1,0:T(4,128)S(1)}, s32[32,128]{1,0:T(8,12...) custom-call(s32[1]{0:T(128)} %bitcast.rank_ref, ...), custom_call_target="tpu_custom_call" | custom-call | flops 2000000000 | bytes 1048576 | tf_op jit(solution)/shard_map/pallas_call | solution.py:667
  3.6 6.1 %all-to-all-start = ((bf16[32,40,128]{2,1,0:T(8,128)(2,1)}), bf16[32,40,128]{2,1,0:T(8,128)(2,1)S(1)}, u32[]{:S(2)}, u32[]{:S(2)}) async-start(bf16[32,40,128]{2,1,0:T(8,128)(2,1)} %get-tuple-element.31), calls=%async_computation | async-start | bytes 655360 | tf_op jit(solution)/shard_map/all_to_all | solution.py:618
  9.7 0.2 collective-permute-start
  10.0 6.1 %collective-permute-start.1 = (bf16[64,128]{1,0:T(8,128)(2,1)S(1)}, bf16[64,128]{1,0:T(8,128)(2,1)S(1)}, u32[]{:S(2)}, u32[]{:S(2)}) collective-permute-start(bf16[64,128]{1,0:T(8,128)(2,1)S(1)} %get-tuple-element.38), channel_id=1, source_target_pairs={{1,2},{2,1},{3,4},{4,3},{5,6},{6,5},{7,8},{8,7},{9,10},{10,9},{11,... | collective-permute-start | bytes 49160 | tf_op jit(solution)/shard_map/ppermute | solution.py:607
  16.1 6.2 %shard_map.105 = (f32[64,2048]{1,0:T(8,128)S(1)}, f32[64,2048]{1,0:T(8,128)S(1)}) custom-call(s32[1]{0:T(128)} %bitcast.rank_ref, f32[32]{0:T(128)} %coef_ref.11, f32[64,2048]{1,0:T(8,128)} %field_ref.3, f32[64,2048]{1,0:T(8,128)} %rhs_ref.1, f32[1,2048]{1,0:T(1,128)S(1)} %get-tuple-element.32.mass_ref, s32[32,128]{1,0:T(8,128)S(1)} %get-tuple-element.33.keys_ref, ...), custom_call_target="tpu_custom_call" | custom-call | flops 5000000000 | bytes 1048576 | tf_op jit(solution)/shard_map/pallas_call | solution.py:629
  22.3 0.0 collective-permute-done.first_ref
  22.3 0.0 collective-permute-done.1.second_ref
  22.3 0.0 all-to-all-done.chunk_ref
  22.3 0.4 shard_map.106
  22.7 0.1 collective-permute-start.2
  22.8 3.1 %collective-permute-start.3 = (bf16[64,128]{1,0:T(8,128)(2,1)S(1)}, bf16[64,128]{1,0:T(8,128)(2,1)S(1)}, u32[]{:S(2)}, u32[]{:S(2)}) collective-permute-start(bf16[64,128]{1,0:T(8,128)(2,1)S(1)} %get-tuple-element.42), channel_id=1, source_target_pairs={{1,2},{2,1},{3,4},{4,3},{5,6},{6,5},{7,8},{8,7},{9,10},{10,9},{11,... | collective-permute-start | bytes 49160 | tf_op jit(solution)/shard_map/ppermute | solution.py:607
  25.9 8.3 %shard_map.109 = (f32[8,64,192]{2,1,0:T(8,128)}, bf16[4,2,192,1536]{3,2,1,0:T(8,128)(2,1)}) custom-call(s32[1]{0:T(128)} %bitcast.rank_ref, s32[3,768]{1,0:T(4,128)S(1)} %get-tuple-element.43.map_ref, bf16[32,40,128]{2,1,0:T(8,128)(2,1)S(1)} %all-to-all-done.chunk_ref), custom_call_target="tpu_custom_call" | custom-call | flops 8000000000 | bytes 1048576 | tf_op jit(solution)/shard_map/pallas_call | solution.py:694
  34.2 3.7 %all-to-all-start.1 = ((f32[8,64,192]{2,1,0:T(8,128)}), f32[8,64,192]{2,1,0:T(8,128)S(1)}, u32[]{:S(2)}, u32[]{:S(2)}) async-start(f32[8,64,192]{2,1,0:T(8,128)} %get-tuple-element.44), calls=%async_computation.1 | async-start | bytes 1048576 | tf_op jit(solution)/shard_map/all_to_all | solution.py:664
  37.9 5.7 %shard_map.107.field_ref = f32[64,2048]{1,0:T(8,128)S(1)} custom-call(s32[1]{0:T(128)} %bitcast.rank_ref, f32[32]{0:T(128)} %coef_ref.11, f32[64,2048]{1,0:T(8,128)S(1)} %get-tuple-element.39.field_ref, f32[64,2048]{1,0:T(8,128)S(1)} %get-tuple-element.40.rhs_ref, f32[1,2048]{1,0:T(1,128)S(1)} %get-tuple-element.32.mass_ref, ...), custom_call_target="tpu_custom_call" | custom-call | flops 5000000000 | bytes 1048576 | tf_op jit(solution)/shard_map/pallas_call | solution.py:629
  43.6 0.0 collective-permute-done.2.more_refs_0_
  43.6 0.0 collective-permute-done.3.more_refs_1_
  43.6 7.3 %collective-permute-start.5 = (bf16[64,128]{1,0:T(8,128)(2,1)S(1)}, bf16[64,128]{1,0:T(8,128)(2,1)S(1)}, u32[]{:S(2)}, u32[]{:S(2)}) collective-permute-start(bf16[64,128]{1,0:T(8,128)(2,1)S(1)} %get-tuple-element.56), channel_id=1, source_target_pairs={{1,2},{2,1},{3,4},{4,3},{5,6},{6,5},{7,8},{8,7},{9,10},{10,9},{11,... | collective-permute-start | bytes 49160 | tf_op jit(solution)/shard_map/ppermute | solution.py:607
  50.9 0.1 collective-permute-start.4
  51.0 5.7 %shard_map.108.field_ref = f32[64,2048]{1,0:T(8,128)S(1)} custom-call(s32[1]{0:T(128)} %bitcast.rank_ref, f32[32]{0:T(128)} %coef_ref.11, f32[64,2048]{1,0:T(8,128)S(1)} %shard_map.107.field_ref, f32[64,2048]{1,0:T(8,128)S(1)} %get-tuple-element.40.rhs_ref, f32[1,2048]{1,0:T(1,128)S(1)} %get-tuple-element.32.mass_ref, ...), custom_call_target="tpu_custom_call" | custom-call | flops 5000000000 | bytes 1048576 | tf_op jit(solution)/shard_map/pallas_call | solution.py:629
  56.7 0.0 collective-permute-done.5.second_ref
  56.7 0.0 collective-permute-done.4.first_ref
  56.7 0.0 all-to-all-done.1.parts_ref
  56.7 1.3 %shard_map.110 = (f32[64,2048]{1,0:T(8,128)S(1)}, bf16[32,32,128]{2,1,0:T(8,128)(2,1)}, bf16[64,128]{1,0:T(8,128)(2,1)S(1)}, bf16[64,128]{1,0:T(8,128)(2,1)S(1)}) custom-call(s32[1]{0:T(128)} %bitcast.rank_ref, s32[3,192]{1,0:T(4,128)S(1)} %get-tuple-element.29.own_map_ref, s32[8,384]{1,0:T(8,128)S(1)} %get-tuple-element.30.nodes_ref, ...), custom_call_target="tpu_custom_call" | custom-call | flops 1000000000 | bytes 1048576 | tf_op jit(solution)/shard_map/pallas_call | solution.py:718
  58.1 2.3 %all-to-all-start.2 = ((bf16[32,32,128]{2,1,0:T(8,128)(2,1)}), bf16[32,32,128]{2,1,0:T(8,128)(2,1)S(1)}, u32[]{:S(2)}, u32[]{:S(2)}) async-start(bf16[32,32,128]{2,1,0:T(8,128)(2,1)} %get-tuple-element.45), calls=%async_computation.2 | async-start | bytes 524288 | tf_op jit(solution)/shard_map/all_to_all | solution.py:618
  60.4 0.6 collective-permute-start.6
  61.0 5.9 %collective-permute-start.7 = (bf16[64,128]{1,0:T(8,128)(2,1)S(1)}, bf16[64,128]{1,0:T(8,128)(2,1)S(1)}, u32[]{:S(2)}, u32[]{:S(2)}) collective-permute-start(bf16[64,128]{1,0:T(8,128)(2,1)S(1)} %get-tuple-element.48), channel_id=1, source_target_pairs={{1,2},{2,1},{3,4},{4,3},{5,6},{6,5},{7,8},{8,7},{9,10},{10,9},{11,... | collective-permute-start | bytes 49160 | tf_op jit(solution)/shard_map/ppermute | solution.py:607
  66.8 5.7 %shard_map.111.field_ref = f32[64,2048]{1,0:T(8,128)S(1)} custom-call(s32[1]{0:T(128)} %bitcast.rank_ref, f32[32]{0:T(128)} %coef_ref.11, f32[64,2048]{1,0:T(8,128)S(1)} %get-tuple-element.46.field_ref, f32[64,2048]{1,0:T(8,128)S(1)} %get-tuple-element.35.forcing_ref.rhs_ref, f32[1,2048]{1,0:T(1,128)S(1)} %get-tuple-element.32.mass_ref, ...), custom_call_target="tpu_custom_call" | custom-call | flops 5000000000 | bytes 1048576 | tf_op jit(solution)/shard_map/pallas_call | solution.py:629
  72.5 0.0 all-to-all-done.2.chunk_ref
  72.6 3.7 %shard_map.115 = f32[8,64,192]{2,1,0:T(8,128)} custom-call(s32[3,768]{1,0:T(4,128)S(1)} %get-tuple-element.43.map_ref, bf16[32,32,128]{2,1,0:T(8,128)(2,1)S(1)} %all-to-all-done.2.chunk_ref, bf16[4,2,192,1536]{3,2,1,0:T(8,128)(2,1)} %get-tuple-element.53.tile_ref), custom_call_target="tpu_custom_call" | custom-call | flops 2000000000 | bytes 1048576 | tf_op jit(solution)/shard_map/pallas_call | solution.py:729
  76.3 3.5 %all-to-all-start.3 = ((f32[8,64,192]{2,1,0:T(8,128)}), f32[8,64,192]{2,1,0:T(8,128)S(1)}, u32[]{:S(2)}, u32[]{:S(2)}) async-start(f32[8,64,192]{2,1,0:T(8,128)} %shard_map.115), calls=%async_computation.3 | async-start | bytes 1048576 | tf_op jit(solution)/shard_map/all_to_all | solution.py:664
  79.8 0.0 collective-permute-done.6.first_ref
  79.8 0.0 collective-permute-done.7.second_ref
  79.8 0.4 shard_map.112
  80.2 0.5 collective-permute-start.8
  80.7 5.3 %collective-permute-start.9 = (bf16[64,128]{1,0:T(8,128)(2,1)S(1)}, bf16[64,128]{1,0:T(8,128)(2,1)S(1)}, u32[]{:S(2)}, u32[]{:S(2)}) collective-permute-start(bf16[64,128]{1,0:T(8,128)(2,1)S(1)} %get-tuple-element.52), channel_id=1, source_target_pairs={{1,2},{2,1},{3,4},{4,3},{5,6},{6,5},{7,8},{8,7},{9,10},{10,9},{11,... | collective-permute-start | bytes 49160 | tf_op jit(solution)/shard_map/ppermute | solution.py:607
  86.0 5.7 %shard_map.113.field_ref = f32[64,2048]{1,0:T(8,128)S(1)} custom-call(s32[1]{0:T(128)} %bitcast.rank_ref, f32[32]{0:T(128)} %coef_ref.11, f32[64,2048]{1,0:T(8,128)S(1)} %get-tuple-element.49.field_ref, f32[64,2048]{1,0:T(8,128)S(1)} %get-tuple-element.50.rhs_ref, f32[1,2048]{1,0:T(1,128)S(1)} %get-tuple-element.32.mass_ref, ...), custom_call_target="tpu_custom_call" | custom-call | flops 5000000000 | bytes 1048576 | tf_op jit(solution)/shard_map/pallas_call | solution.py:629
  91.8 0.0 collective-permute-done.8.more_refs_0_
  91.8 1.4 %collective-permute-done.9.more_refs_1_ = bf16[64,128]{1,0:T(8,128)(2,1)S(1)} collective-permute-done((bf16[64,128]{1,0:T(8,128)(2,1)S(1)}, bf16[64,128]{1,0:T(8,128)(2,1)S(1)}, u32[]{:S(2)}, u32[]{:S(2)}) %collective-permute-start.9) | collective-permute-done | bytes 16416 | tf_op jit(solution)/shard_map/ppermute | solution.py:607
  93.2 4.1 %collective-permute-start.11 = (bf16[64,128]{1,0:T(8,128)(2,1)S(1)}, bf16[64,128]{1,0:T(8,128)(2,1)S(1)}, u32[]{:S(2)}, u32[]{:S(2)}) collective-permute-start(bf16[64,128]{1,0:T(8,128)(2,1)S(1)} %get-tuple-element.54), channel_id=1, source_target_pairs={{1,2},{2,1},{3,4},{4,3},{5,6},{6,5},{7,8},{8,7},{9,10},{10,9},{11,... | collective-permute-start | bytes 49160 | tf_op jit(solution)/shard_map/ppermute | solution.py:607
  97.3 0.1 collective-permute-start.10
  97.4 5.7 %shard_map.114.field_ref = f32[64,2048]{1,0:T(8,128)S(1)} custom-call(s32[1]{0:T(128)} %bitcast.rank_ref, f32[32]{0:T(128)} %coef_ref.11, f32[64,2048]{1,0:T(8,128)S(1)} %shard_map.113.field_ref, f32[64,2048]{1,0:T(8,128)S(1)} %get-tuple-element.50.rhs_ref, f32[1,2048]{1,0:T(1,128)S(1)} %get-tuple-element.32.mass_ref, ...), custom_call_target="tpu_custom_call" | custom-call | flops 5000000000 | bytes 1048576 | tf_op jit(solution)/shard_map/pallas_call | solution.py:629
  103.1 0.0 collective-permute-done.11.second_ref
  103.1 0.0 collective-permute-done.10.first_ref
  103.2 0.0 all-to-all-done.3.parts_ref
  103.2 0.9 shard_map.116
  (3 shorter events, 0.0 us)
Async XLA Ops:
  3.6 18.7 %all-to-all-start = ((bf16[32,40,128]{2,1,0:T(8,128)(2,1)}), bf16[32,40,128]{2,1,0:T(8,128)(2,1)S(1)}, u32[]{:S(2)}, u32[]{:S(2)}) async-start(bf16[32,40,128]{2,1,0:T(8,128)(2,1)} %get-tuple-element.31), calls=%async_computation | async-start | bytes 655360 | tf_op jit(solution)/shard_map/all_to_all | solution.py:618
  9.7 12.5 %collective-permute-start = (bf16[64,128]{1,0:T(8,128)(2,1)S(1)}, bf16[64,128]{1,0:T(8,128)(2,1)S(1)}, u32[]{:S(2)}, u32[]{:S(2)}) collective-permute-start(bf16[64,128]{1,0:T(8,128)(2,1)S(1)} %get-tuple-element.37), channel_id=1, source_target_pairs={{0,1},{1,0},{2,3},{3,2},{4,5},{5,4},{6,7},{7,6},{8,9},{9,8},{10,11... | collective-permute-start | bytes 49160 | tf_op jit(solution)/shard_map/ppermute | solution.py:607
  10.0 12.3 %collective-permute-start.1 = (bf16[64,128]{1,0:T(8,128)(2,1)S(1)}, bf16[64,128]{1,0:T(8,128)(2,1)S(1)}, u32[]{:S(2)}, u32[]{:S(2)}) collective-permute-start(bf16[64,128]{1,0:T(8,128)(2,1)S(1)} %get-tuple-element.38), channel_id=1, source_target_pairs={{1,2},{2,1},{3,4},{4,3},{5,6},{6,5},{7,8},{8,7},{9,10},{10,9},{11,... | collective-permute-start | bytes 49160 | tf_op jit(solution)/shard_map/ppermute | solution.py:607
  22.7 20.8 %collective-permute-start.2 = (bf16[64,128]{1,0:T(8,128)(2,1)S(1)}, bf16[64,128]{1,0:T(8,128)(2,1)S(1)}, u32[]{:S(2)}, u32[]{:S(2)}) collective-permute-start(bf16[64,128]{1,0:T(8,128)(2,1)S(1)} %get-tuple-element.41), channel_id=1, source_target_pairs={{0,1},{1,0},{2,3},{3,2},{4,5},{5,4},{6,7},{7,6},{8,9},{9,8},{10,11... | collective-permute-start | bytes 49160 | tf_op jit(solution)/shard_map/ppermute | solution.py:607
  22.8 20.8 %collective-permute-start.3 = (bf16[64,128]{1,0:T(8,128)(2,1)S(1)}, bf16[64,128]{1,0:T(8,128)(2,1)S(1)}, u32[]{:S(2)}, u32[]{:S(2)}) collective-permute-start(bf16[64,128]{1,0:T(8,128)(2,1)S(1)} %get-tuple-element.42), channel_id=1, source_target_pairs={{1,2},{2,1},{3,4},{4,3},{5,6},{6,5},{7,8},{8,7},{9,10},{10,9},{11,... | collective-permute-start | bytes 49160 | tf_op jit(solution)/shard_map/ppermute | solution.py:607
  34.2 22.5 %all-to-all-start.1 = ((f32[8,64,192]{2,1,0:T(8,128)}), f32[8,64,192]{2,1,0:T(8,128)S(1)}, u32[]{:S(2)}, u32[]{:S(2)}) async-start(f32[8,64,192]{2,1,0:T(8,128)} %get-tuple-element.44), calls=%async_computation.1 | async-start | bytes 1048576 | tf_op jit(solution)/shard_map/all_to_all | solution.py:664
  43.6 13.1 %collective-permute-start.5 = (bf16[64,128]{1,0:T(8,128)(2,1)S(1)}, bf16[64,128]{1,0:T(8,128)(2,1)S(1)}, u32[]{:S(2)}, u32[]{:S(2)}) collective-permute-start(bf16[64,128]{1,0:T(8,128)(2,1)S(1)} %get-tuple-element.56), channel_id=1, source_target_pairs={{1,2},{2,1},{3,4},{4,3},{5,6},{6,5},{7,8},{8,7},{9,10},{10,9},{11,... | collective-permute-start | bytes 49160 | tf_op jit(solution)/shard_map/ppermute | solution.py:607
  50.9 5.8 %collective-permute-start.4 = (bf16[64,128]{1,0:T(8,128)(2,1)S(1)}, bf16[64,128]{1,0:T(8,128)(2,1)S(1)}, u32[]{:S(2)}, u32[]{:S(2)}) collective-permute-start(bf16[64,128]{1,0:T(8,128)(2,1)S(1)} %get-tuple-element.57), channel_id=1, source_target_pairs={{0,1},{1,0},{2,3},{3,2},{4,5},{5,4},{6,7},{7,6},{8,9},{9,8},{10,11... | collective-permute-start | bytes 49160 | tf_op jit(solution)/shard_map/ppermute | solution.py:607
  58.1 14.5 %all-to-all-start.2 = ((bf16[32,32,128]{2,1,0:T(8,128)(2,1)}), bf16[32,32,128]{2,1,0:T(8,128)(2,1)S(1)}, u32[]{:S(2)}, u32[]{:S(2)}) async-start(bf16[32,32,128]{2,1,0:T(8,128)(2,1)} %get-tuple-element.45), calls=%async_computation.2 | async-start | bytes 524288 | tf_op jit(solution)/shard_map/all_to_all | solution.py:618
  60.4 19.4 %collective-permute-start.6 = (bf16[64,128]{1,0:T(8,128)(2,1)S(1)}, bf16[64,128]{1,0:T(8,128)(2,1)S(1)}, u32[]{:S(2)}, u32[]{:S(2)}) collective-permute-start(bf16[64,128]{1,0:T(8,128)(2,1)S(1)} %get-tuple-element.47), channel_id=1, source_target_pairs={{0,1},{1,0},{2,3},{3,2},{4,5},{5,4},{6,7},{7,6},{8,9},{9,8},{10,11... | collective-permute-start | bytes 49160 | tf_op jit(solution)/shard_map/ppermute | solution.py:607
  61.0 18.8 %collective-permute-start.7 = (bf16[64,128]{1,0:T(8,128)(2,1)S(1)}, bf16[64,128]{1,0:T(8,128)(2,1)S(1)}, u32[]{:S(2)}, u32[]{:S(2)}) collective-permute-start(bf16[64,128]{1,0:T(8,128)(2,1)S(1)} %get-tuple-element.48), channel_id=1, source_target_pairs={{1,2},{2,1},{3,4},{4,3},{5,6},{6,5},{7,8},{8,7},{9,10},{10,9},{11,... | collective-permute-start | bytes 49160 | tf_op jit(solution)/shard_map/ppermute | solution.py:607
  76.3 26.9 %all-to-all-start.3 = ((f32[8,64,192]{2,1,0:T(8,128)}), f32[8,64,192]{2,1,0:T(8,128)S(1)}, u32[]{:S(2)}, u32[]{:S(2)}) async-start(f32[8,64,192]{2,1,0:T(8,128)} %shard_map.115), calls=%async_computation.3 | async-start | bytes 1048576 | tf_op jit(solution)/shard_map/all_to_all | solution.py:664
  80.2 11.5 %collective-permute-start.8 = (bf16[64,128]{1,0:T(8,128)(2,1)S(1)}, bf16[64,128]{1,0:T(8,128)(2,1)S(1)}, u32[]{:S(2)}, u32[]{:S(2)}) collective-permute-start(bf16[64,128]{1,0:T(8,128)(2,1)S(1)} %get-tuple-element.51), channel_id=1, source_target_pairs={{0,1},{1,0},{2,3},{3,2},{4,5},{5,4},{6,7},{7,6},{8,9},{9,8},{10,11... | collective-permute-start | bytes 49160 | tf_op jit(solution)/shard_map/ppermute | solution.py:607
  80.7 12.5 %collective-permute-start.9 = (bf16[64,128]{1,0:T(8,128)(2,1)S(1)}, bf16[64,128]{1,0:T(8,128)(2,1)S(1)}, u32[]{:S(2)}, u32[]{:S(2)}) collective-permute-start(bf16[64,128]{1,0:T(8,128)(2,1)S(1)} %get-tuple-element.52), channel_id=1, source_target_pairs={{1,2},{2,1},{3,4},{4,3},{5,6},{6,5},{7,8},{8,7},{9,10},{10,9},{11,... | collective-permute-start | bytes 49160 | tf_op jit(solution)/shard_map/ppermute | solution.py:607
  93.2 9.9 %collective-permute-start.11 = (bf16[64,128]{1,0:T(8,128)(2,1)S(1)}, bf16[64,128]{1,0:T(8,128)(2,1)S(1)}, u32[]{:S(2)}, u32[]{:S(2)}) collective-permute-start(bf16[64,128]{1,0:T(8,128)(2,1)S(1)} %get-tuple-element.54), channel_id=1, source_target_pairs={{1,2},{2,1},{3,4},{4,3},{5,6},{6,5},{7,8},{8,7},{9,10},{10,9},{11,... | collective-permute-start | bytes 49160 | tf_op jit(solution)/shard_map/ppermute | solution.py:607
  97.3 5.8 %collective-permute-start.10 = (bf16[64,128]{1,0:T(8,128)(2,1)S(1)}, bf16[64,128]{1,0:T(8,128)(2,1)S(1)}, u32[]{:S(2)}, u32[]{:S(2)}) collective-permute-start(bf16[64,128]{1,0:T(8,128)(2,1)S(1)} %get-tuple-element.55), channel_id=1, source_target_pairs={{0,1},{1,0},{2,3},{3,2},{4,5},{5,4},{6,7},{7,6},{8,9},{9,8},{10,11... | collective-permute-start | bytes 49160 | tf_op jit(solution)/shard_map/ppermute | solution.py:607
where the time goes:
time: 105 us; the launch traced here: 104 us
  Pallas kernels  52.8 us (50%)
  starting transfers between devices  48.8 us (46%)
  waiting for transfers between devices  1.43 us (1%)
    pallas_call x6, Pallas kernels, sweep(): call(functools.partial(sweep_kernel, parts, weight, weight_before, keep),...  34.7 us
    ppermute x6, starting transfers between devices, exchange(): lax.ppermute(second, AXES, odd_pairs)  31.8 us
    all_to_all x2, starting transfers between devices, swap_all(): return lax.all_to_all(chunks, AXES, split_axis=0, concat_axis=0, tiled=True)  8.43 us
    pallas_call x1, Pallas kernels, per_device(): call(functools.partial(tile_kernel, *sizes), (parts_shape, pltpu.HBM(tile...  8.29 us
    all_to_all x2, starting transfers between devices, swap_parts(): lax.all_to_all(parts_out, 'bcol', split_axis=0, concat_axis=0, tiled=True)  7.21 us
    pallas_call x1, Pallas kernels, per_device(): call(functools.partial(potential_kernel, *sizes), parts_shape, 2000000000...  3.72 us
    pallas_call x1, Pallas kernels, per_device(): call(functools.partial(setup_kernel, parts, brow, bcol, panel_dev, slot_r...  3 us
  transfers between devices with their start and end apart: 16, of which 1 were waited for; matrix products, arithmetic and copies ran while one was open for 0% of the time, Pallas kernels for 45%

commit v1 on v0

--- a/solution.py
+++ b/solution.py
@@ -14,7 +14,7 @@
 LOAD_ROWS = 8
 POINT_ROWS = 8
 HALVES = 2
-GROUP = 4
+GROUP = 8
 BLOCKS = 4
 
 wave_number = 20.0
@@ -222,7 +222,7 @@
     parts, brow, bcol, panel_dev, slot_rows, rank_ref, map_ref, field_ref, potential_ref, points_ref,
     element_nodes_ref, element_matrix_ref, node_mass_ref,
     nodes_ref, load_nodes_ref, source_map_ref, own_map_ref, keys_ref, matrix_ref, mass_ref,
-    chunk_ref, rim_first_ref, rim_second_ref,
+    field_kept_ref, chunk_ref, rim_first_ref, rim_second_ref,
 ):
     rank = rank_ref[0]
     source_map_ref[...] = jnp.concatenate(
@@ -243,6 +243,7 @@
     nodes_ref[...] = jnp.broadcast_to(nodes, nodes_ref.shape)
     load_nodes_ref[...] = jnp.broadcast_to(load_nodes, load_nodes_ref.shape)
     field = field_ref[...]
+    field_kept_ref[...] = field
     write_rims(field, low_part(rank, 2) == 0, rim_first_ref, rim_second_ref)
     loads = load_rows(potential_ref[...], own_map, brow * bcol, slot_rows)
     pieces = trace_rows(field, nodes, parts, bcol, brow * slot_rows)
@@ -624,7 +625,7 @@
     def sweep(field, rhs, weight, halo=(), weight_before=None, keep=False):
         rows = parts * columns
         lanes = GROUP * LANES
-        large = in_hbm(field, rhs) if keep else (field, rhs)
+        large = (*in_vmem(field), *in_hbm(rhs)) if keep else (field, rhs)
         given = (rank, *in_hbm(element_coef), *large, *in_vmem(mass, keys, matrix), *halo)
         return call(
             functools.partial(sweep_kernel, parts, weight, weight_before, keep),
@@ -664,7 +665,7 @@
         return lax.all_to_all(parts_out, "bcol", split_axis=0, concat_axis=0, tiled=True)
 
     trace_slots, load_slots = table_lanes(brow, bcol, slot_rows)
-    (nodes, load_nodes, source_map, own_map, keys, matrix, mass, chunks, *rim) = call(
+    (nodes, load_nodes, source_map, own_map, keys, matrix, mass, field_kept, chunks, *rim) = call(
         functools.partial(setup_kernel, parts, brow, bcol, panel_dev, slot_rows),
         (
             kept((8, trace_slots), jnp.int32),
@@ -674,13 +675,14 @@
             kept((elements, LANES), jnp.int32),
             kept((LANES, LANES), F32),
             kept((1, count), F32),
+            kept((columns, count), F32),
             chunk_shape(used + LOAD_ROWS + POINT_ROWS, 8),
             kept(rim_shape.shape, BF16),
             kept(rim_shape.shape, BF16),
         ),
         2_000_000_000,
         in_specs=[smem] + [vmem] * 7,
-        out_specs=(vmem,) * 10,
+        out_specs=(vmem,) * 11,
     )(
         rank,
         *in_hbm(
@@ -690,7 +692,7 @@
     )
     halo = exchange(*rim)
     chunks = swap_all(chunks)
-    field, forcing_kept = sweep(field_start, forcing, weights[0], keep=True)
+    field, forcing_kept = sweep(field_kept, forcing, weights[0], keep=True)
     parts_out, tiles = call(
         functools.partial(tile_kernel, *sizes),
         (parts_shape, pltpu.HBM(tile_shape, BF16)),

time: 105 us -> 109 us (1.038)
  Pallas kernels: 52.8 us -> 57.3 us
    pallas_call x6, Pallas kernels: 34.7 us -> 39.2 us  [sweep(): call(functools.partial(sweep_kernel, parts, weight, weight_before, keep),...]
  transfers between devices with their start and end apart: 16 -> 16, of which waited for: 1 -> 1; matrix products, arithmetic and copies ran while one was open for 0% -> 0% of each run, Pallas kernels for 45% -> 48%
where the time goes in v1:
time: 109 us; the launch traced here: 108 us
  Pallas kernels  57.3 us (53%)
  starting transfers between devices  48.8 us (45%)
    pallas_call x6, Pallas kernels, sweep(): call(functools.partial(sweep_kernel, parts, weight, weight_before, keep),...  39.2 us
    ppermute x6, starting transfers between devices, exchange(): lax.ppermute(second, AXES, odd_pairs)  31.7 us
    all_to_all x2, starting transfers between devices, swap_all(): return lax.all_to_all(chunks, AXES, split_axis=0, concat_axis=0, tiled=True)  8.42 us
    pallas_call x1, Pallas kernels, per_device(): call(functools.partial(tile_kernel, *sizes), (parts_shape, pltpu.HBM(tile...  8.3 us
    all_to_all x2, starting transfers between devices, swap_parts(): lax.all_to_all(parts_out, 'bcol', split_axis=0, concat_axis=0, tiled=True)  7.21 us
    pallas_call x1, Pallas kernels, per_device(): call(functools.partial(potential_kernel, *sizes), parts_shape, 2000000000...  3.72 us
    pallas_call x1, Pallas kernels, per_device(): call(functools.partial(setup_kernel, parts, brow, bcol, panel_dev, slot_r...  3.02 us
  transfers between devices with their start and end apart: 16, of which 1 were waited for; matrix products, arithmetic and copies ran while one was open for 0% of the time, Pallas kernels for 48%

profile of v1, /device:TPU:4, one launch (start us, length us, event | category | flops | bytes accessed | tf_op | source)
XLA Modules:
  0.0 107.8 jit_solution(4284435959182796742)
XLA Ops:
  0.6 3.0 %shard_map.104 = (s32[8,384]{1,0:T(8,128)S(1)}, s32[8,512]{1,0:T(8,128)S(1)}, s32[3,768]{1,0:T(4,128)S(1)}, s32[3,192]{1,0:T(4,128)S(1)}, s32[32,128]{1,0:T(8,12...) custom-call(s32[1]{0:T(128)} %bitcast.rank_ref, ...), custom_call_target="tpu_custom_call" | custom-call | flops 2000000000 | bytes 1048576 | tf_op jit(solution)/shard_map/pallas_call | solution.py:668
  3.7 6.1 %all-to-all-start = ((bf16[32,40,128]{2,1,0:T(8,128)(2,1)}), bf16[32,40,128]{2,1,0:T(8,128)(2,1)S(1)}, u32[]{:S(2)}, u32[]{:S(2)}) async-start(bf16[32,40,128]{2,1,0:T(8,128)(2,1)} %get-tuple-element.32), calls=%async_computation | async-start | bytes 655360 | tf_op jit(solution)/shard_map/all_to_all | solution.py:619
  9.8 0.2 collective-permute-start
  10.0 6.1 %collective-permute-start.1 = (bf16[64,128]{1,0:T(8,128)(2,1)S(1)}, bf16[64,128]{1,0:T(8,128)(2,1)S(1)}, u32[]{:S(2)}, u32[]{:S(2)}) collective-permute-start(bf16[64,128]{1,0:T(8,128)(2,1)S(1)} %get-tuple-element.40), channel_id=1, source_target_pairs={{1,2},{2,1},{3,4},{4,3},{5,6},{6,5},{7,8},{8,7},{9,10},{10,9},{11,... | collective-permute-start | bytes 49160 | tf_op jit(solution)/shard_map/ppermute | solution.py:608
  16.1 6.6 %shard_map.105 = (f32[64,2048]{1,0:T(8,128)S(1)}, f32[64,2048]{1,0:T(8,128)S(1)}) custom-call(s32[1]{0:T(128)} %bitcast.rank_ref, f32[32]{0:T(128)} %coef_ref.11, f32[64,2048]{1,0:T(8,128)S(1)} %get-tuple-element.33.field_ref, f32[64,2048]{1,0:T(8,128)} %rhs_ref.1, f32[1,2048]{1,0:T(1,128)S(1)} %get-tuple-element.34.mass_ref, ...), custom_call_target="tpu_custom_call" | custom-call | flops 5000000000 | bytes 1048576 | tf_op jit(solution)/shard_map/pallas_call | solution.py:630
  22.7 0.0 collective-permute-done.first_ref
  22.8 0.0 collective-permute-done.1.second_ref
  22.8 0.0 all-to-all-done.chunk_ref
  22.8 0.4 shard_map.106
  23.2 0.1 collective-permute-start.2
  23.3 3.1 %collective-permute-start.3 = (bf16[64,128]{1,0:T(8,128)(2,1)S(1)}, bf16[64,128]{1,0:T(8,128)(2,1)S(1)}, u32[]{:S(2)}, u32[]{:S(2)}) collective-permute-start(bf16[64,128]{1,0:T(8,128)(2,1)S(1)} %get-tuple-element.44), channel_id=1, source_target_pairs={{1,2},{2,1},{3,4},{4,3},{5,6},{6,5},{7,8},{8,7},{9,10},{10,9},{11,... | collective-permute-start | bytes 49160 | tf_op jit(solution)/shard_map/ppermute | solution.py:608
  26.3 8.3 %shard_map.109 = (f32[8,64,192]{2,1,0:T(8,128)}, bf16[4,2,192,1536]{3,2,1,0:T(8,128)(2,1)}) custom-call(s32[1]{0:T(128)} %bitcast.rank_ref, s32[3,768]{1,0:T(4,128)S(1)} %get-tuple-element.45.map_ref, bf16[32,40,128]{2,1,0:T(8,128)(2,1)S(1)} %all-to-all-done.chunk_ref), custom_call_target="tpu_custom_call" | custom-call | flops 8000000000 | bytes 1048576 | tf_op jit(solution)/shard_map/pallas_call | solution.py:696
  34.6 3.7 %all-to-all-start.1 = ((f32[8,64,192]{2,1,0:T(8,128)}), f32[8,64,192]{2,1,0:T(8,128)S(1)}, u32[]{:S(2)}, u32[]{:S(2)}) async-start(f32[8,64,192]{2,1,0:T(8,128)} %get-tuple-element.46), calls=%async_computation.1 | async-start | bytes 1048576 | tf_op jit(solution)/shard_map/all_to_all | solution.py:665
  38.4 6.5 %shard_map.107.field_ref = f32[64,2048]{1,0:T(8,128)S(1)} custom-call(s32[1]{0:T(128)} %bitcast.rank_ref, f32[32]{0:T(128)} %coef_ref.11, f32[64,2048]{1,0:T(8,128)S(1)} %get-tuple-element.41.field_ref, f32[64,2048]{1,0:T(8,128)S(1)} %get-tuple-element.42.rhs_ref, f32[1,2048]{1,0:T(1,128)S(1)} %get-tuple-element.34.mass_ref, ...), custom_call_target="tpu_custom_call" | custom-call | flops 5000000000 | bytes 1048576 | tf_op jit(solution)/shard_map/pallas_call | solution.py:630
  44.9 0.0 collective-permute-done.2.more_refs_0_
  44.9 0.0 collective-permute-done.3.more_refs_1_
  44.9 7.3 %collective-permute-start.5 = (bf16[64,128]{1,0:T(8,128)(2,1)S(1)}, bf16[64,128]{1,0:T(8,128)(2,1)S(1)}, u32[]{:S(2)}, u32[]{:S(2)}) collective-permute-start(bf16[64,128]{1,0:T(8,128)(2,1)S(1)} %get-tuple-element.58), channel_id=1, source_target_pairs={{1,2},{2,1},{3,4},{4,3},{5,6},{6,5},{7,8},{8,7},{9,10},{10,9},{11,... | collective-permute-start | bytes 49160 | tf_op jit(solution)/shard_map/ppermute | solution.py:608
  52.2 0.1 collective-permute-start.4
  52.3 6.5 %shard_map.108.field_ref = f32[64,2048]{1,0:T(8,128)S(1)} custom-call(s32[1]{0:T(128)} %bitcast.rank_ref, f32[32]{0:T(128)} %coef_ref.11, f32[64,2048]{1,0:T(8,128)S(1)} %shard_map.107.field_ref, f32[64,2048]{1,0:T(8,128)S(1)} %get-tuple-element.42.rhs_ref, f32[1,2048]{1,0:T(1,128)S(1)} %get-tuple-element.34.mass_ref, ...), custom_call_target="tpu_custom_call" | custom-call | flops 5000000000 | bytes 1048576 | tf_op jit(solution)/shard_map/pallas_call | solution.py:630
  58.8 0.0 collective-permute-done.5.second_ref
  58.8 0.0 collective-permute-done.4.first_ref
  58.8 0.0 all-to-all-done.1.parts_ref
  58.8 1.3 %shard_map.110 = (f32[64,2048]{1,0:T(8,128)S(1)}, bf16[32,32,128]{2,1,0:T(8,128)(2,1)}, bf16[64,128]{1,0:T(8,128)(2,1)S(1)}, bf16[64,128]{1,0:T(8,128)(2,1)S(1)}) custom-call(s32[1]{0:T(128)} %bitcast.rank_ref, s32[3,192]{1,0:T(4,128)S(1)} %get-tuple-element.30.own_map_ref, s32[8,384]{1,0:T(8,128)S(1)} %get-tuple-element.31.nodes_ref, ...), custom_call_target="tpu_custom_call" | custom-call | flops 1000000000 | bytes 1048576 | tf_op jit(solution)/shard_map/pallas_call | solution.py:720
  60.2 2.3 %all-to-all-start.2 = ((bf16[32,32,128]{2,1,0:T(8,128)(2,1)}), bf16[32,32,128]{2,1,0:T(8,128)(2,1)S(1)}, u32[]{:S(2)}, u32[]{:S(2)}) async-start(bf16[32,32,128]{2,1,0:T(8,128)(2,1)} %get-tuple-element.47), calls=%async_computation.2 | async-start | bytes 524288 | tf_op jit(solution)/shard_map/all_to_all | solution.py:619
  62.5 0.6 collective-permute-start.6
  63.1 5.9 %collective-permute-start.7 = (bf16[64,128]{1,0:T(8,128)(2,1)S(1)}, bf16[64,128]{1,0:T(8,128)(2,1)S(1)}, u32[]{:S(2)}, u32[]{:S(2)}) collective-permute-start(bf16[64,128]{1,0:T(8,128)(2,1)S(1)} %get-tuple-element.50), channel_id=1, source_target_pairs={{1,2},{2,1},{3,4},{4,3},{5,6},{6,5},{7,8},{8,7},{9,10},{10,9},{11,... | collective-permute-start | bytes 49160 | tf_op jit(solution)/shard_map/ppermute | solution.py:608
  68.9 6.5 %shard_map.111.field_ref = f32[64,2048]{1,0:T(8,128)S(1)} custom-call(s32[1]{0:T(128)} %bitcast.rank_ref, f32[32]{0:T(128)} %coef_ref.11, f32[64,2048]{1,0:T(8,128)S(1)} %get-tuple-element.48.field_ref, f32[64,2048]{1,0:T(8,128)S(1)} %get-tuple-element.37.forcing_ref.rhs_ref, f32[1,2048]{1,0:T(1,128)S(1)} %get-tuple-element.34.mass_ref, ...), custom_call_target="tpu_custom_call" | custom-call | flops 5000000000 | bytes 1048576 | tf_op jit(solution)/shard_map/pallas_call | solution.py:630
  75.5 0.0 all-to-all-done.2.chunk_ref
  75.5 3.7 %shard_map.115 = f32[8,64,192]{2,1,0:T(8,128)} custom-call(s32[3,768]{1,0:T(4,128)S(1)} %get-tuple-element.45.map_ref, bf16[32,32,128]{2,1,0:T(8,128)(2,1)S(1)} %all-to-all-done.2.chunk_ref, bf16[4,2,192,1536]{3,2,1,0:T(8,128)(2,1)} %get-tuple-element.55.tile_ref), custom_call_target="tpu_custom_call" | custom-call | flops 2000000000 | bytes 1048576 | tf_op jit(solution)/shard_map/pallas_call | solution.py:731
  79.2 3.5 %all-to-all-start.3 = ((f32[8,64,192]{2,1,0:T(8,128)}), f32[8,64,192]{2,1,0:T(8,128)S(1)}, u32[]{:S(2)}, u32[]{:S(2)}) async-start(f32[8,64,192]{2,1,0:T(8,128)} %shard_map.115), calls=%async_computation.3 | async-start | bytes 1048576 | tf_op jit(solution)/shard_map/all_to_all | solution.py:665
  82.7 0.0 collective-permute-done.6.first_ref
  82.7 0.0 collective-permute-done.7.second_ref
  82.8 0.4 shard_map.112
  83.2 0.5 collective-permute-start.8
  83.6 5.3 %collective-permute-start.9 = (bf16[64,128]{1,0:T(8,128)(2,1)S(1)}, bf16[64,128]{1,0:T(8,128)(2,1)S(1)}, u32[]{:S(2)}, u32[]{:S(2)}) collective-permute-start(bf16[64,128]{1,0:T(8,128)(2,1)S(1)} %get-tuple-element.54), channel_id=1, source_target_pairs={{1,2},{2,1},{3,4},{4,3},{5,6},{6,5},{7,8},{8,7},{9,10},{10,9},{11,... | collective-permute-start | bytes 49160 | tf_op jit(solution)/shard_map/ppermute | solution.py:608
  89.0 6.5 %shard_map.113.field_ref = f32[64,2048]{1,0:T(8,128)S(1)} custom-call(s32[1]{0:T(128)} %bitcast.rank_ref, f32[32]{0:T(128)} %coef_ref.11, f32[64,2048]{1,0:T(8,128)S(1)} %get-tuple-element.51.field_ref, f32[64,2048]{1,0:T(8,128)S(1)} %get-tuple-element.52.rhs_ref, f32[1,2048]{1,0:T(1,128)S(1)} %get-tuple-element.34.mass_ref, ...), custom_call_target="tpu_custom_call" | custom-call | flops 5000000000 | bytes 1048576 | tf_op jit(solution)/shard_map/pallas_call | solution.py:630
  95.5 0.0 collective-permute-done.8.more_refs_0_
  95.5 0.6 collective-permute-done.9.more_refs_1_
  96.1 4.1 %collective-permute-start.11 = (bf16[64,128]{1,0:T(8,128)(2,1)S(1)}, bf16[64,128]{1,0:T(8,128)(2,1)S(1)}, u32[]{:S(2)}, u32[]{:S(2)}) collective-permute-start(bf16[64,128]{1,0:T(8,128)(2,1)S(1)} %get-tuple-element.56), channel_id=1, source_target_pairs={{1,2},{2,1},{3,4},{4,3},{5,6},{6,5},{7,8},{8,7},{9,10},{10,9},{11,... | collective-permute-start | bytes 49160 | tf_op jit(solution)/shard_map/ppermute | solution.py:608
  100.3 0.1 collective-permute-start.10
  100.3 6.5 %shard_map.114.field_ref = f32[64,2048]{1,0:T(8,128)S(1)} custom-call(s32[1]{0:T(128)} %bitcast.rank_ref, f32[32]{0:T(128)} %coef_ref.11, f32[64,2048]{1,0:T(8,128)S(1)} %shard_map.113.field_ref, f32[64,2048]{1,0:T(8,128)S(1)} %get-tuple-element.52.rhs_ref, f32[1,2048]{1,0:T(1,128)S(1)} %get-tuple-element.34.mass_ref, ...), custom_call_target="tpu_custom_call" | custom-call | flops 5000000000 | bytes 1048576 | tf_op jit(solution)/shard_map/pallas_call | solution.py:630
  106.9 0.0 collective-permute-done.11.second_ref
  106.9 0.0 collective-permute-done.10.first_ref
  106.9 0.0 all-to-all-done.3.parts_ref
  106.9 0.9 shard_map.116
  (3 shorter events, 0.0 us)
Async XLA Ops:
  3.7 19.1 %all-to-all-start = ((bf16[32,40,128]{2,1,0:T(8,128)(2,1)}), bf16[32,40,128]{2,1,0:T(8,128)(2,1)S(1)}, u32[]{:S(2)}, u32[]{:S(2)}) async-start(bf16[32,40,128]{2,1,0:T(8,128)(2,1)} %get-tuple-element.32), calls=%async_computation | async-start | bytes 655360 | tf_op jit(solution)/shard_map/all_to_all | solution.py:619
  9.8 13.0 %collective-permute-start = (bf16[64,128]{1,0:T(8,128)(2,1)S(1)}, bf16[64,128]{1,0:T(8,128)(2,1)S(1)}, u32[]{:S(2)}, u32[]{:S(2)}) collective-permute-start(bf16[64,128]{1,0:T(8,128)(2,1)S(1)} %get-tuple-element.39), channel_id=1, source_target_pairs={{0,1},{1,0},{2,3},{3,2},{4,5},{5,4},{6,7},{7,6},{8,9},{9,8},{10,11... | collective-permute-start | bytes 49160 | tf_op jit(solution)/shard_map/ppermute | solution.py:608
  10.0 12.8 %collective-permute-start.1 = (bf16[64,128]{1,0:T(8,128)(2,1)S(1)}, bf16[64,128]{1,0:T(8,128)(2,1)S(1)}, u32[]{:S(2)}, u32[]{:S(2)}) collective-permute-start(bf16[64,128]{1,0:T(8,128)(2,1)S(1)} %get-tuple-element.40), channel_id=1, source_target_pairs={{1,2},{2,1},{3,4},{4,3},{5,6},{6,5},{7,8},{8,7},{9,10},{10,9},{11,... | collective-permute-start | bytes 49160 | tf_op jit(solution)/shard_map/ppermute | solution.py:608
  23.2 21.7 %collective-permute-start.2 = (bf16[64,128]{1,0:T(8,128)(2,1)S(1)}, bf16[64,128]{1,0:T(8,128)(2,1)S(1)}, u32[]{:S(2)}, u32[]{:S(2)}) collective-permute-start(bf16[64,128]{1,0:T(8,128)(2,1)S(1)} %get-tuple-element.43), channel_id=1, source_target_pairs={{0,1},{1,0},{2,3},{3,2},{4,5},{5,4},{6,7},{7,6},{8,9},{9,8},{10,11... | collective-permute-start | bytes 49160 | tf_op jit(solution)/shard_map/ppermute | solution.py:608
  23.3 21.6 %collective-permute-start.3 = (bf16[64,128]{1,0:T(8,128)(2,1)S(1)}, bf16[64,128]{1,0:T(8,128)(2,1)S(1)}, u32[]{:S(2)}, u32[]{:S(2)}) collective-permute-start(bf16[64,128]{1,0:T(8,128)(2,1)S(1)} %get-tuple-element.44), channel_id=1, source_target_pairs={{1,2},{2,1},{3,4},{4,3},{5,6},{6,5},{7,8},{8,7},{9,10},{10,9},{11,... | collective-permute-start | bytes 49160 | tf_op jit(solution)/shard_map/ppermute | solution.py:608
  34.6 24.2 %all-to-all-start.1 = ((f32[8,64,192]{2,1,0:T(8,128)}), f32[8,64,192]{2,1,0:T(8,128)S(1)}, u32[]{:S(2)}, u32[]{:S(2)}) async-start(f32[8,64,192]{2,1,0:T(8,128)} %get-tuple-element.46), calls=%async_computation.1 | async-start | bytes 1048576 | tf_op jit(solution)/shard_map/all_to_all | solution.py:665
  44.9 13.9 %collective-permute-start.5 = (bf16[64,128]{1,0:T(8,128)(2,1)S(1)}, bf16[64,128]{1,0:T(8,128)(2,1)S(1)}, u32[]{:S(2)}, u32[]{:S(2)}) collective-permute-start(bf16[64,128]{1,0:T(8,128)(2,1)S(1)} %get-tuple-element.58), channel_id=1, source_target_pairs={{1,2},{2,1},{3,4},{4,3},{5,6},{6,5},{7,8},{8,7},{9,10},{10,9},{11,... | collective-permute-start | bytes 49160 | tf_op jit(solution)/shard_map/ppermute | solution.py:608
  52.2 6.6 %collective-permute-start.4 = (bf16[64,128]{1,0:T(8,128)(2,1)S(1)}, bf16[64,128]{1,0:T(8,128)(2,1)S(1)}, u32[]{:S(2)}, u32[]{:S(2)}) collective-permute-start(bf16[64,128]{1,0:T(8,128)(2,1)S(1)} %get-tuple-element.59), channel_id=1, source_target_pairs={{0,1},{1,0},{2,3},{3,2},{4,5},{5,4},{6,7},{7,6},{8,9},{9,8},{10,11... | collective-permute-start | bytes 49160 | tf_op jit(solution)/shard_map/ppermute | solution.py:608
  60.2 15.3 %all-to-all-start.2 = ((bf16[32,32,128]{2,1,0:T(8,128)(2,1)}), bf16[32,32,128]{2,1,0:T(8,128)(2,1)S(1)}, u32[]{:S(2)}, u32[]{:S(2)}) async-start(bf16[32,32,128]{2,1,0:T(8,128)(2,1)} %get-tuple-element.47), calls=%async_computation.2 | async-start | bytes 524288 | tf_op jit(solution)/shard_map/all_to_all | solution.py:619
  62.5 20.2 %collective-permute-start.6 = (bf16[64,128]{1,0:T(8,128)(2,1)S(1)}, bf16[64,128]{1,0:T(8,128)(2,1)S(1)}, u32[]{:S(2)}, u32[]{:S(2)}) collective-permute-start(bf16[64,128]{1,0:T(8,128)(2,1)S(1)} %get-tuple-element.49), channel_id=1, source_target_pairs={{0,1},{1,0},{2,3},{3,2},{4,5},{5,4},{6,7},{7,6},{8,9},{9,8},{10,11... | collective-permute-start | bytes 49160 | tf_op jit(solution)/shard_map/ppermute | solution.py:608
  63.1 19.7 %collective-permute-start.7 = (bf16[64,128]{1,0:T(8,128)(2,1)S(1)}, bf16[64,128]{1,0:T(8,128)(2,1)S(1)}, u32[]{:S(2)}, u32[]{:S(2)}) collective-permute-start(bf16[64,128]{1,0:T(8,128)(2,1)S(1)} %get-tuple-element.50), channel_id=1, source_target_pairs={{1,2},{2,1},{3,4},{4,3},{5,6},{6,5},{7,8},{8,7},{9,10},{10,9},{11,... | collective-permute-start | bytes 49160 | tf_op jit(solution)/shard_map/ppermute | solution.py:608
  79.2 27.7 %all-to-all-start.3 = ((f32[8,64,192]{2,1,0:T(8,128)}), f32[8,64,192]{2,1,0:T(8,128)S(1)}, u32[]{:S(2)}, u32[]{:S(2)}) async-start(f32[8,64,192]{2,1,0:T(8,128)} %shard_map.115), calls=%async_computation.3 | async-start | bytes 1048576 | tf_op jit(solution)/shard_map/all_to_all | solution.py:665
  83.2 12.3 %collective-permute-start.8 = (bf16[64,128]{1,0:T(8,128)(2,1)S(1)}, bf16[64,128]{1,0:T(8,128)(2,1)S(1)}, u32[]{:S(2)}, u32[]{:S(2)}) collective-permute-start(bf16[64,128]{1,0:T(8,128)(2,1)S(1)} %get-tuple-element.53), channel_id=1, source_target_pairs={{0,1},{1,0},{2,3},{3,2},{4,5},{5,4},{6,7},{7,6},{8,9},{9,8},{10,11... | collective-permute-start | bytes 49160 | tf_op jit(solution)/shard_map/ppermute | solution.py:608
  83.6 12.5 %collective-permute-start.9 = (bf16[64,128]{1,0:T(8,128)(2,1)S(1)}, bf16[64,128]{1,0:T(8,128)(2,1)S(1)}, u32[]{:S(2)}, u32[]{:S(2)}) collective-permute-start(bf16[64,128]{1,0:T(8,128)(2,1)S(1)} %get-tuple-element.54), channel_id=1, source_target_pairs={{1,2},{2,1},{3,4},{4,3},{5,6},{6,5},{7,8},{8,7},{9,10},{10,9},{11,... | collective-permute-start | bytes 49160 | tf_op jit(solution)/shard_map/ppermute | solution.py:608
  96.1 10.7 %collective-permute-start.11 = (bf16[64,128]{1,0:T(8,128)(2,1)S(1)}, bf16[64,128]{1,0:T(8,128)(2,1)S(1)}, u32[]{:S(2)}, u32[]{:S(2)}) collective-permute-start(bf16[64,128]{1,0:T(8,128)(2,1)S(1)} %get-tuple-element.56), channel_id=1, source_target_pairs={{1,2},{2,1},{3,4},{4,3},{5,6},{6,5},{7,8},{8,7},{9,10},{10,9},{11,... | collective-permute-start | bytes 49160 | tf_op jit(solution)/shard_map/ppermute | solution.py:608
  100.3 6.6 %collective-permute-start.10 = (bf16[64,128]{1,0:T(8,128)(2,1)S(1)}, bf16[64,128]{1,0:T(8,128)(2,1)S(1)}, u32[]{:S(2)}, u32[]{:S(2)}) collective-permute-start(bf16[64,128]{1,0:T(8,128)(2,1)S(1)} %get-tuple-element.57), channel_id=1, source_target_pairs={{0,1},{1,0},{2,3},{3,2},{4,5},{5,4},{6,7},{7,6},{8,9},{9,8},{10,11... | collective-permute-start | bytes 49160 | tf_op jit(solution)/shard_map/ppermute | solution.py:608

commit v2 on v1

--- a/solution.py
+++ b/solution.py
@@ -14,7 +14,7 @@
 LOAD_ROWS = 8
 POINT_ROWS = 8
 HALVES = 2
-GROUP = 8
+GROUP = 4
 BLOCKS = 4
 
 wave_number = 20.0

time: 109 us -> 105 us (0.963)
  Pallas kernels: 57.3 us -> 52.4 us
    pallas_call x6, Pallas kernels: 39.2 us -> 34.3 us  [sweep(): call(functools.partial(sweep_kernel, parts, weight, weight_before, keep),...]
  transfers between devices with their start and end apart: 16 -> 16, of which waited for: 1 -> 1; matrix products, arithmetic and copies ran while one was open for 0% -> 0% of each run, Pallas kernels for 48% -> 45%
where the time goes in v2:
time: 105 us; the launch traced here: 104 us
  Pallas kernels  52.4 us (50%)
  starting transfers between devices  48.8 us (46%)
  waiting for transfers between devices  1.43 us (1%)
    pallas_call x6, Pallas kernels, sweep(): call(functools.partial(sweep_kernel, parts, weight, weight_before, keep),...  34.3 us
    ppermute x6, starting transfers between devices, exchange(): lax.ppermute(second, AXES, odd_pairs)  31.8 us
    all_to_all x2, starting transfers between devices, swap_all(): return lax.all_to_all(chunks, AXES, split_axis=0, concat_axis=0, tiled=True)  8.42 us
    pallas_call x1, Pallas kernels, per_device(): call(functools.partial(tile_kernel, *sizes), (parts_shape, pltpu.HBM(tile...  8.29 us
    all_to_all x2, starting transfers between devices, swap_parts(): lax.all_to_all(parts_out, 'bcol', split_axis=0, concat_axis=0, tiled=True)  7.22 us
    pallas_call x1, Pallas kernels, per_device(): call(functools.partial(potential_kernel, *sizes), parts_shape, 2000000000...  3.72 us
    pallas_call x1, Pallas kernels, per_device(): call(functools.partial(setup_kernel, parts, brow, bcol, panel_dev, slot_r...  3.02 us
  transfers between devices with their start and end apart: 16, of which 1 were waited for; matrix products, arithmetic and copies ran while one was open for 0% of the time, Pallas kernels for 45%

profile of v2, /device:TPU:4, one launch (start us, length us, event | category | flops | bytes accessed | tf_op | source)
XLA Modules:
  0.0 103.7 jit_solution(10245223003940509687)
XLA Ops:
  0.6 3.0 %shard_map.104 = (s32[8,384]{1,0:T(8,128)S(1)}, s32[8,512]{1,0:T(8,128)S(1)}, s32[3,768]{1,0:T(4,128)S(1)}, s32[3,192]{1,0:T(4,128)S(1)}, s32[32,128]{1,0:T(8,12...) custom-call(s32[1]{0:T(128)} %bitcast.rank_ref, ...), custom_call_target="tpu_custom_call" | custom-call | flops 2000000000 | bytes 1048576 | tf_op jit(solution)/shard_map/pallas_call | solution.py:668
  3.7 6.1 %all-to-all-start = ((bf16[32,40,128]{2,1,0:T(8,128)(2,1)}), bf16[32,40,128]{2,1,0:T(8,128)(2,1)S(1)}, u32[]{:S(2)}, u32[]{:S(2)}) async-start(bf16[32,40,128]{2,1,0:T(8,128)(2,1)} %get-tuple-element.32), calls=%async_computation | async-start | bytes 655360 | tf_op jit(solution)/shard_map/all_to_all | solution.py:619
  9.8 0.2 collective-permute-start
  10.0 6.1 %collective-permute-start.1 = (bf16[64,128]{1,0:T(8,128)(2,1)S(1)}, bf16[64,128]{1,0:T(8,128)(2,1)S(1)}, u32[]{:S(2)}, u32[]{:S(2)}) collective-permute-start(bf16[64,128]{1,0:T(8,128)(2,1)S(1)} %get-tuple-element.40), channel_id=1, source_target_pairs={{1,2},{2,1},{3,4},{4,3},{5,6},{6,5},{7,8},{8,7},{9,10},{10,9},{11,... | collective-permute-start | bytes 49160 | tf_op jit(solution)/shard_map/ppermute | solution.py:608
  16.1 5.8 %shard_map.105 = (f32[64,2048]{1,0:T(8,128)S(1)}, f32[64,2048]{1,0:T(8,128)S(1)}) custom-call(s32[1]{0:T(128)} %bitcast.rank_ref, f32[32]{0:T(128)} %coef_ref.11, f32[64,2048]{1,0:T(8,128)S(1)} %get-tuple-element.33.field_ref, f32[64,2048]{1,0:T(8,128)} %rhs_ref.1, f32[1,2048]{1,0:T(1,128)S(1)} %get-tuple-element.34.mass_ref, ...), custom_call_target="tpu_custom_call" | custom-call | flops 5000000000 | bytes 1048576 | tf_op jit(solution)/shard_map/pallas_call | solution.py:630
  21.9 0.0 collective-permute-done.first_ref
  21.9 0.0 collective-permute-done.1.second_ref
  21.9 0.0 all-to-all-done.chunk_ref
  21.9 0.4 shard_map.106
  22.4 0.1 collective-permute-start.2
  22.4 3.1 %collective-permute-start.3 = (bf16[64,128]{1,0:T(8,128)(2,1)S(1)}, bf16[64,128]{1,0:T(8,128)(2,1)S(1)}, u32[]{:S(2)}, u32[]{:S(2)}) collective-permute-start(bf16[64,128]{1,0:T(8,128)(2,1)S(1)} %get-tuple-element.44), channel_id=1, source_target_pairs={{1,2},{2,1},{3,4},{4,3},{5,6},{6,5},{7,8},{8,7},{9,10},{10,9},{11,... | collective-permute-start | bytes 49160 | tf_op jit(solution)/shard_map/ppermute | solution.py:608
  25.5 8.3 %shard_map.109 = (f32[8,64,192]{2,1,0:T(8,128)}, bf16[4,2,192,1536]{3,2,1,0:T(8,128)(2,1)}) custom-call(s32[1]{0:T(128)} %bitcast.rank_ref, s32[3,768]{1,0:T(4,128)S(1)} %get-tuple-element.45.map_ref, bf16[32,40,128]{2,1,0:T(8,128)(2,1)S(1)} %all-to-all-done.chunk_ref), custom_call_target="tpu_custom_call" | custom-call | flops 8000000000 | bytes 1048576 | tf_op jit(solution)/shard_map/pallas_call | solution.py:696
  33.8 3.7 %all-to-all-start.1 = ((f32[8,64,192]{2,1,0:T(8,128)}), f32[8,64,192]{2,1,0:T(8,128)S(1)}, u32[]{:S(2)}, u32[]{:S(2)}) async-start(f32[8,64,192]{2,1,0:T(8,128)} %get-tuple-element.46), calls=%async_computation.1 | async-start | bytes 1048576 | tf_op jit(solution)/shard_map/all_to_all | solution.py:665
  37.5 5.7 %shard_map.107.field_ref = f32[64,2048]{1,0:T(8,128)S(1)} custom-call(s32[1]{0:T(128)} %bitcast.rank_ref, f32[32]{0:T(128)} %coef_ref.11, f32[64,2048]{1,0:T(8,128)S(1)} %get-tuple-element.41.field_ref, f32[64,2048]{1,0:T(8,128)S(1)} %get-tuple-element.42.rhs_ref, f32[1,2048]{1,0:T(1,128)S(1)} %get-tuple-element.34.mass_ref, ...), custom_call_target="tpu_custom_call" | custom-call | flops 5000000000 | bytes 1048576 | tf_op jit(solution)/shard_map/pallas_call | solution.py:630
  43.2 0.0 collective-permute-done.2.more_refs_0_
  43.2 0.0 collective-permute-done.3.more_refs_1_
  43.3 7.3 %collective-permute-start.5 = (bf16[64,128]{1,0:T(8,128)(2,1)S(1)}, bf16[64,128]{1,0:T(8,128)(2,1)S(1)}, u32[]{:S(2)}, u32[]{:S(2)}) collective-permute-start(bf16[64,128]{1,0:T(8,128)(2,1)S(1)} %get-tuple-element.58), channel_id=1, source_target_pairs={{1,2},{2,1},{3,4},{4,3},{5,6},{6,5},{7,8},{8,7},{9,10},{10,9},{11,... | collective-permute-start | bytes 49160 | tf_op jit(solution)/shard_map/ppermute | solution.py:608
  50.5 0.1 collective-permute-start.4
  50.6 5.7 %shard_map.108.field_ref = f32[64,2048]{1,0:T(8,128)S(1)} custom-call(s32[1]{0:T(128)} %bitcast.rank_ref, f32[32]{0:T(128)} %coef_ref.11, f32[64,2048]{1,0:T(8,128)S(1)} %shard_map.107.field_ref, f32[64,2048]{1,0:T(8,128)S(1)} %get-tuple-element.42.rhs_ref, f32[1,2048]{1,0:T(1,128)S(1)} %get-tuple-element.34.mass_ref, ...), custom_call_target="tpu_custom_call" | custom-call | flops 5000000000 | bytes 1048576 | tf_op jit(solution)/shard_map/pallas_call | solution.py:630
  56.3 0.0 collective-permute-done.5.second_ref
  56.4 0.0 collective-permute-done.4.first_ref
  56.4 0.0 all-to-all-done.1.parts_ref
  56.4 1.3 %shard_map.110 = (f32[64,2048]{1,0:T(8,128)S(1)}, bf16[32,32,128]{2,1,0:T(8,128)(2,1)}, bf16[64,128]{1,0:T(8,128)(2,1)S(1)}, bf16[64,128]{1,0:T(8,128)(2,1)S(1)}) custom-call(s32[1]{0:T(128)} %bitcast.rank_ref, s32[3,192]{1,0:T(4,128)S(1)} %get-tuple-element.30.own_map_ref, s32[8,384]{1,0:T(8,128)S(1)} %get-tuple-element.31.nodes_ref, ...), custom_call_target="tpu_custom_call" | custom-call | flops 1000000000 | bytes 1048576 | tf_op jit(solution)/shard_map/pallas_call | solution.py:720
  57.7 2.3 %all-to-all-start.2 = ((bf16[32,32,128]{2,1,0:T(8,128)(2,1)}), bf16[32,32,128]{2,1,0:T(8,128)(2,1)S(1)}, u32[]{:S(2)}, u32[]{:S(2)}) async-start(bf16[32,32,128]{2,1,0:T(8,128)(2,1)} %get-tuple-element.47), calls=%async_computation.2 | async-start | bytes 524288 | tf_op jit(solution)/shard_map/all_to_all | solution.py:619
  60.0 0.6 collective-permute-start.6
  60.6 5.9 %collective-permute-start.7 = (bf16[64,128]{1,0:T(8,128)(2,1)S(1)}, bf16[64,128]{1,0:T(8,128)(2,1)S(1)}, u32[]{:S(2)}, u32[]{:S(2)}) collective-permute-start(bf16[64,128]{1,0:T(8,128)(2,1)S(1)} %get-tuple-element.50), channel_id=1, source_target_pairs={{1,2},{2,1},{3,4},{4,3},{5,6},{6,5},{7,8},{8,7},{9,10},{10,9},{11,... | collective-permute-start | bytes 49160 | tf_op jit(solution)/shard_map/ppermute | solution.py:608
  66.5 5.7 %shard_map.111.field_ref = f32[64,2048]{1,0:T(8,128)S(1)} custom-call(s32[1]{0:T(128)} %bitcast.rank_ref, f32[32]{0:T(128)} %coef_ref.11, f32[64,2048]{1,0:T(8,128)S(1)} %get-tuple-element.48.field_ref, f32[64,2048]{1,0:T(8,128)S(1)} %get-tuple-element.37.forcing_ref.rhs_ref, f32[1,2048]{1,0:T(1,128)S(1)} %get-tuple-element.34.mass_ref, ...), custom_call_target="tpu_custom_call" | custom-call | flops 5000000000 | bytes 1048576 | tf_op jit(solution)/shard_map/pallas_call | solution.py:630
  72.2 0.0 all-to-all-done.2.chunk_ref
  72.2 3.7 %shard_map.115 = f32[8,64,192]{2,1,0:T(8,128)} custom-call(s32[3,768]{1,0:T(4,128)S(1)} %get-tuple-element.45.map_ref, bf16[32,32,128]{2,1,0:T(8,128)(2,1)S(1)} %all-to-all-done.2.chunk_ref, bf16[4,2,192,1536]{3,2,1,0:T(8,128)(2,1)} %get-tuple-element.55.tile_ref), custom_call_target="tpu_custom_call" | custom-call | flops 2000000000 | bytes 1048576 | tf_op jit(solution)/shard_map/pallas_call | solution.py:731
  75.9 3.5 %all-to-all-start.3 = ((f32[8,64,192]{2,1,0:T(8,128)}), f32[8,64,192]{2,1,0:T(8,128)S(1)}, u32[]{:S(2)}, u32[]{:S(2)}) async-start(f32[8,64,192]{2,1,0:T(8,128)} %shard_map.115), calls=%async_computation.3 | async-start | bytes 1048576 | tf_op jit(solution)/shard_map/all_to_all | solution.py:665
  79.4 0.0 collective-permute-done.6.first_ref
  79.4 0.0 collective-permute-done.7.second_ref
  79.5 0.4 shard_map.112
  79.9 0.5 collective-permute-start.8
  80.3 5.3 %collective-permute-start.9 = (bf16[64,128]{1,0:T(8,128)(2,1)S(1)}, bf16[64,128]{1,0:T(8,128)(2,1)S(1)}, u32[]{:S(2)}, u32[]{:S(2)}) collective-permute-start(bf16[64,128]{1,0:T(8,128)(2,1)S(1)} %get-tuple-element.54), channel_id=1, source_target_pairs={{1,2},{2,1},{3,4},{4,3},{5,6},{6,5},{7,8},{8,7},{9,10},{10,9},{11,... | collective-permute-start | bytes 49160 | tf_op jit(solution)/shard_map/ppermute | solution.py:608
  85.7 5.7 %shard_map.113.field_ref = f32[64,2048]{1,0:T(8,128)S(1)} custom-call(s32[1]{0:T(128)} %bitcast.rank_ref, f32[32]{0:T(128)} %coef_ref.11, f32[64,2048]{1,0:T(8,128)S(1)} %get-tuple-element.51.field_ref, f32[64,2048]{1,0:T(8,128)S(1)} %get-tuple-element.52.rhs_ref, f32[1,2048]{1,0:T(1,128)S(1)} %get-tuple-element.34.mass_ref, ...), custom_call_target="tpu_custom_call" | custom-call | flops 5000000000 | bytes 1048576 | tf_op jit(solution)/shard_map/pallas_call | solution.py:630
  91.4 0.0 collective-permute-done.8.more_refs_0_
  91.4 1.4 %collective-permute-done.9.more_refs_1_ = bf16[64,128]{1,0:T(8,128)(2,1)S(1)} collective-permute-done((bf16[64,128]{1,0:T(8,128)(2,1)S(1)}, bf16[64,128]{1,0:T(8,128)(2,1)S(1)}, u32[]{:S(2)}, u32[]{:S(2)}) %collective-permute-start.9) | collective-permute-done | bytes 16416 | tf_op jit(solution)/shard_map/ppermute | solution.py:608
  92.8 4.1 %collective-permute-start.11 = (bf16[64,128]{1,0:T(8,128)(2,1)S(1)}, bf16[64,128]{1,0:T(8,128)(2,1)S(1)}, u32[]{:S(2)}, u32[]{:S(2)}) collective-permute-start(bf16[64,128]{1,0:T(8,128)(2,1)S(1)} %get-tuple-element.56), channel_id=1, source_target_pairs={{1,2},{2,1},{3,4},{4,3},{5,6},{6,5},{7,8},{8,7},{9,10},{10,9},{11,... | collective-permute-start | bytes 49160 | tf_op jit(solution)/shard_map/ppermute | solution.py:608
  97.0 0.1 collective-permute-start.10
  97.0 5.7 %shard_map.114.field_ref = f32[64,2048]{1,0:T(8,128)S(1)} custom-call(s32[1]{0:T(128)} %bitcast.rank_ref, f32[32]{0:T(128)} %coef_ref.11, f32[64,2048]{1,0:T(8,128)S(1)} %shard_map.113.field_ref, f32[64,2048]{1,0:T(8,128)S(1)} %get-tuple-element.52.rhs_ref, f32[1,2048]{1,0:T(1,128)S(1)} %get-tuple-element.34.mass_ref, ...), custom_call_target="tpu_custom_call" | custom-call | flops 5000000000 | bytes 1048576 | tf_op jit(solution)/shard_map/pallas_call | solution.py:630
  102.8 0.0 collective-permute-done.11.second_ref
  102.8 0.0 collective-permute-done.10.first_ref
  102.8 0.0 all-to-all-done.3.parts_ref
  102.8 0.9 shard_map.116
  (3 shorter events, 0.0 us)
Async XLA Ops:
  3.7 18.3 %all-to-all-start = ((bf16[32,40,128]{2,1,0:T(8,128)(2,1)}), bf16[32,40,128]{2,1,0:T(8,128)(2,1)S(1)}, u32[]{:S(2)}, u32[]{:S(2)}) async-start(bf16[32,40,128]{2,1,0:T(8,128)(2,1)} %get-tuple-element.32), calls=%async_computation | async-start | bytes 655360 | tf_op jit(solution)/shard_map/all_to_all | solution.py:619
  9.8 12.2 %collective-permute-start = (bf16[64,128]{1,0:T(8,128)(2,1)S(1)}, bf16[64,128]{1,0:T(8,128)(2,1)S(1)}, u32[]{:S(2)}, u32[]{:S(2)}) collective-permute-start(bf16[64,128]{1,0:T(8,128)(2,1)S(1)} %get-tuple-element.39), channel_id=1, source_target_pairs={{0,1},{1,0},{2,3},{3,2},{4,5},{5,4},{6,7},{7,6},{8,9},{9,8},{10,11... | collective-permute-start | bytes 49160 | tf_op jit(solution)/shard_map/ppermute | solution.py:608
  10.0 11.9 %collective-permute-start.1 = (bf16[64,128]{1,0:T(8,128)(2,1)S(1)}, bf16[64,128]{1,0:T(8,128)(2,1)S(1)}, u32[]{:S(2)}, u32[]{:S(2)}) collective-permute-start(bf16[64,128]{1,0:T(8,128)(2,1)S(1)} %get-tuple-element.40), channel_id=1, source_target_pairs={{1,2},{2,1},{3,4},{4,3},{5,6},{6,5},{7,8},{8,7},{9,10},{10,9},{11,... | collective-permute-start | bytes 49160 | tf_op jit(solution)/shard_map/ppermute | solution.py:608
  22.4 20.8 %collective-permute-start.2 = (bf16[64,128]{1,0:T(8,128)(2,1)S(1)}, bf16[64,128]{1,0:T(8,128)(2,1)S(1)}, u32[]{:S(2)}, u32[]{:S(2)}) collective-permute-start(bf16[64,128]{1,0:T(8,128)(2,1)S(1)} %get-tuple-element.43), channel_id=1, source_target_pairs={{0,1},{1,0},{2,3},{3,2},{4,5},{5,4},{6,7},{7,6},{8,9},{9,8},{10,11... | collective-permute-start | bytes 49160 | tf_op jit(solution)/shard_map/ppermute | solution.py:608
  22.4 20.8 %collective-permute-start.3 = (bf16[64,128]{1,0:T(8,128)(2,1)S(1)}, bf16[64,128]{1,0:T(8,128)(2,1)S(1)}, u32[]{:S(2)}, u32[]{:S(2)}) collective-permute-start(bf16[64,128]{1,0:T(8,128)(2,1)S(1)} %get-tuple-element.44), channel_id=1, source_target_pairs={{1,2},{2,1},{3,4},{4,3},{5,6},{6,5},{7,8},{8,7},{9,10},{10,9},{11,... | collective-permute-start | bytes 49160 | tf_op jit(solution)/shard_map/ppermute | solution.py:608
  33.8 22.6 %all-to-all-start.1 = ((f32[8,64,192]{2,1,0:T(8,128)}), f32[8,64,192]{2,1,0:T(8,128)S(1)}, u32[]{:S(2)}, u32[]{:S(2)}) async-start(f32[8,64,192]{2,1,0:T(8,128)} %get-tuple-element.46), calls=%async_computation.1 | async-start | bytes 1048576 | tf_op jit(solution)/shard_map/all_to_all | solution.py:665
  43.3 13.1 %collective-permute-start.5 = (bf16[64,128]{1,0:T(8,128)(2,1)S(1)}, bf16[64,128]{1,0:T(8,128)(2,1)S(1)}, u32[]{:S(2)}, u32[]{:S(2)}) collective-permute-start(bf16[64,128]{1,0:T(8,128)(2,1)S(1)} %get-tuple-element.58), channel_id=1, source_target_pairs={{1,2},{2,1},{3,4},{4,3},{5,6},{6,5},{7,8},{8,7},{9,10},{10,9},{11,... | collective-permute-start | bytes 49160 | tf_op jit(solution)/shard_map/ppermute | solution.py:608
  50.5 5.8 %collective-permute-start.4 = (bf16[64,128]{1,0:T(8,128)(2,1)S(1)}, bf16[64,128]{1,0:T(8,128)(2,1)S(1)}, u32[]{:S(2)}, u32[]{:S(2)}) collective-permute-start(bf16[64,128]{1,0:T(8,128)(2,1)S(1)} %get-tuple-element.59), channel_id=1, source_target_pairs={{0,1},{1,0},{2,3},{3,2},{4,5},{5,4},{6,7},{7,6},{8,9},{9,8},{10,11... | collective-permute-start | bytes 49160 | tf_op jit(solution)/shard_map/ppermute | solution.py:608
  57.7 14.5 %all-to-all-start.2 = ((bf16[32,32,128]{2,1,0:T(8,128)(2,1)}), bf16[32,32,128]{2,1,0:T(8,128)(2,1)S(1)}, u32[]{:S(2)}, u32[]{:S(2)}) async-start(bf16[32,32,128]{2,1,0:T(8,128)(2,1)} %get-tuple-element.47), calls=%async_computation.2 | async-start | bytes 524288 | tf_op jit(solution)/shard_map/all_to_all | solution.py:619
  60.0 19.4 %collective-permute-start.6 = (bf16[64,128]{1,0:T(8,128)(2,1)S(1)}, bf16[64,128]{1,0:T(8,128)(2,1)S(1)}, u32[]{:S(2)}, u32[]{:S(2)}) collective-permute-start(bf16[64,128]{1,0:T(8,128)(2,1)S(1)} %get-tuple-element.49), channel_id=1, source_target_pairs={{0,1},{1,0},{2,3},{3,2},{4,5},{5,4},{6,7},{7,6},{8,9},{9,8},{10,11... | collective-permute-start | bytes 49160 | tf_op jit(solution)/shard_map/ppermute | solution.py:608
  60.6 18.8 %collective-permute-start.7 = (bf16[64,128]{1,0:T(8,128)(2,1)S(1)}, bf16[64,128]{1,0:T(8,128)(2,1)S(1)}, u32[]{:S(2)}, u32[]{:S(2)}) collective-permute-start(bf16[64,128]{1,0:T(8,128)(2,1)S(1)} %get-tuple-element.50), channel_id=1, source_target_pairs={{1,2},{2,1},{3,4},{4,3},{5,6},{6,5},{7,8},{8,7},{9,10},{10,9},{11,... | collective-permute-start | bytes 49160 | tf_op jit(solution)/shard_map/ppermute | solution.py:608
  75.9 26.9 %all-to-all-start.3 = ((f32[8,64,192]{2,1,0:T(8,128)}), f32[8,64,192]{2,1,0:T(8,128)S(1)}, u32[]{:S(2)}, u32[]{:S(2)}) async-start(f32[8,64,192]{2,1,0:T(8,128)} %shard_map.115), calls=%async_computation.3 | async-start | bytes 1048576 | tf_op jit(solution)/shard_map/all_to_all | solution.py:665
  79.9 11.5 %collective-permute-start.8 = (bf16[64,128]{1,0:T(8,128)(2,1)S(1)}, bf16[64,128]{1,0:T(8,128)(2,1)S(1)}, u32[]{:S(2)}, u32[]{:S(2)}) collective-permute-start(bf16[64,128]{1,0:T(8,128)(2,1)S(1)} %get-tuple-element.53), channel_id=1, source_target_pairs={{0,1},{1,0},{2,3},{3,2},{4,5},{5,4},{6,7},{7,6},{8,9},{9,8},{10,11... | collective-permute-start | bytes 49160 | tf_op jit(solution)/shard_map/ppermute | solution.py:608
  80.3 12.5 %collective-permute-start.9 = (bf16[64,128]{1,0:T(8,128)(2,1)S(1)}, bf16[64,128]{1,0:T(8,128)(2,1)S(1)}, u32[]{:S(2)}, u32[]{:S(2)}) collective-permute-start(bf16[64,128]{1,0:T(8,128)(2,1)S(1)} %get-tuple-element.54), channel_id=1, source_target_pairs={{1,2},{2,1},{3,4},{4,3},{5,6},{6,5},{7,8},{8,7},{9,10},{10,9},{11,... | collective-permute-start | bytes 49160 | tf_op jit(solution)/shard_map/ppermute | solution.py:608
  92.8 9.9 %collective-permute-start.11 = (bf16[64,128]{1,0:T(8,128)(2,1)S(1)}, bf16[64,128]{1,0:T(8,128)(2,1)S(1)}, u32[]{:S(2)}, u32[]{:S(2)}) collective-permute-start(bf16[64,128]{1,0:T(8,128)(2,1)S(1)} %get-tuple-element.56), channel_id=1, source_target_pairs={{1,2},{2,1},{3,4},{4,3},{5,6},{6,5},{7,8},{8,7},{9,10},{10,9},{11,... | collective-permute-start | bytes 49160 | tf_op jit(solution)/shard_map/ppermute | solution.py:608
  97.0 5.8 %collective-permute-start.10 = (bf16[64,128]{1,0:T(8,128)(2,1)S(1)}, bf16[64,128]{1,0:T(8,128)(2,1)S(1)}, u32[]{:S(2)}, u32[]{:S(2)}) collective-permute-start(bf16[64,128]{1,0:T(8,128)(2,1)S(1)} %get-tuple-element.57), channel_id=1, source_target_pairs={{0,1},{1,0},{2,3},{3,2},{4,5},{5,4},{6,7},{7,6},{8,9},{9,8},{10,11... | collective-permute-start | bytes 49160 | tf_op jit(solution)/shard_map/ppermute | solution.py:608
